TPU v7x, 32 devices: a whole 2x2x4 slice. The times are simulated.
32 devices in a mesh: los: 16 (over z, y, core), tr: 2 (over x).
Axes of the slice: x: 2, y: 2, z: 4, core: 2. Of those that a mesh axis runs over, the one named last changes fastest.
Arguments:
- density: bfloat16 [256, 2304], P('los', 'tr'), may hold values from -6 to 6
- observed_counts: int32 [256, 2304], P('los', 'tr'), may hold values from 0 to 5
- cell_targets: int32 [256, 2304], P('los', 'tr'), may hold values from 0 to 127
- shift_bins: int32 [256, 18], P('los', 'tr'), may hold values from -111 to 111, as said below
- kernel_first: bfloat16 [27, 32], replicated, may hold values from -1.25 to 1.25
- kernel_second: bfloat16 [864, 32], replicated, may hold values from -0.21875 to 0.21875
- kernel_third: bfloat16 [864, 1], replicated, may hold values from -0.21875 to 0.21875
Outputs:
- redshift_rate: float32 [256, 2304], P('los', 'tr')
- loss: float32 [], replicated
- grad_first: float32 [27, 32], replicated
- grad_second: float32 [864, 32], replicated
- grad_third: float32 [864, 1], replicated
Inputs may be any that keep to these rules, and one draw needn't show every extreme that they name: Take blocks of 16 line-of-sight cells and one half of each plane's tiles along the first transverse dimension (tiles 9 b to 9 b + 8). For a tile at cell l of its block, floor((l + shift_bins) / 16) lies in -6..6: the destination block, counted around the loop. Of one block's 144 tiles at most 24 share a destination block, and exactly 24 do for some destination block of every block.
All inputs are finite; a program needn't handle non-finite values.
Results may differ from a plain program's by a relative error of at most 0.00087.
Values may be sent and summed in bfloat16 or wider, within the bound.
A program may use at most 320 MiB of HBM per device.

v0:
```python
import jax
import jax.numpy as jnp
from jax import lax
from jax.sharding import PartitionSpec as P

NZ = 48
REACH = 6


background = 0.2


def padded_2(array, sides, width):
    for axis, dim in sides:
        size, length = (lax.axis_size(axis), array.shape[dim])
        up = [(i, (i + 1) % size) for i in range(size)]
        down = [(j, i) for i, j in up]
        last = lax.slice_in_dim(array, length - width, length, axis=dim)
        initial = lax.slice_in_dim(array, 0, width, axis=dim)
        before = lax.ppermute(last, axis, up)
        after = lax.ppermute(initial, axis, down)
        array = jnp.concatenate([before, array, after], axis=dim)
    return array


def shifted(array, axis, by):
    size = lax.axis_size(axis)
    return lax.ppermute(array, axis, [(i, (i + by) % size) for i in range(size)])


def close_rims(padded):
    position = lax.axis_index("tr")
    tr_count = lax.axis_size("tr")
    below_keep = (position > 0).astype(padded.dtype)
    above_keep = (position < tr_count - 1).astype(padded.dtype)
    padded = padded.at[:, 0].multiply(below_keep)
    padded = padded.at[:, -1].multiply(above_keep)
    return pad_depth(padded)


def pad_depth(field):
    pad_widths = [(0, 0)] * field.ndim
    pad_widths[2] = (1, 1)
    return jnp.pad(field, pad_widths)


def plane_taps(padded, shift_x, flipped, extent):
    pieces = []
    for shift_y in range(3):
        for shift_z in range(3):
            if flipped:
                anchor = (2 - shift_x, 2 - shift_y, 2 - shift_z)
            else:
                anchor = (shift_x, shift_y, shift_z)
            pieces.append(
                padded[
                    anchor[0] : anchor[0] + extent[0],
                    anchor[1] : anchor[1] + extent[1],
                    anchor[2] : anchor[2] + extent[2],
                ]
            )
    return jnp.concatenate(pieces, axis=-1)


def all_taps(padded, flipped, extent):
    return jnp.concatenate(
        [plane_taps(padded, shift_x, flipped, extent) for shift_x in range(3)], axis=-1
    )


def silu_slope(value):
    sigmoid = jax.nn.sigmoid(value)
    return sigmoid * (1.0 + value * (1.0 - sigmoid))


def contract_rows(left, right):
    return lax.dot_general(
        left, right, (((0,), (0,)), ((), ())), preferred_element_type=jnp.float32
    )


def second_conv(padded, kernel_second, extent, hidden):
    rows_out = extent[0] * extent[1] * extent[2]
    total = jnp.zeros((rows_out, hidden), jnp.float32)
    for shift_x in range(3):
        taps_block = plane_taps(padded, shift_x, False, extent).reshape(rows_out, 9 * hidden)
        total = total + jnp.dot(
            taps_block,
            kernel_second[shift_x * 9 * hidden : (shift_x + 1) * 9 * hidden],
            preferred_element_type=jnp.float32,
        )
    return total


def on_device(
    density, observed_counts, cell_targets, shift_bins, kernel_first, kernel_second, kernel_third
):
    slab_cells = shift_bins.shape[0]
    width_tiles = shift_bins.shape[1]
    plane_cells = density.shape[1]
    depth_cells = NZ
    rows_y = plane_cells // depth_cells
    hidden = kernel_second.shape[1]
    extent = (slab_cells, rows_y, depth_cells)
    cell_rows = slab_cells * rows_y * depth_cells
    total_cells = slab_cells * lax.axis_size("los") * plane_cells * lax.axis_size("tr")
    tile_total = slab_cells * width_tiles
    spread = 2 * REACH + 1
    third_matrix = kernel_third.reshape(27, hidden)
    field = density.reshape(slab_cells, rows_y, depth_cells, 1)
    field_pad = close_rims(padded_2(field, (("los", 0), ("tr", 1)), 1))
    first_taps = all_taps(field_pad, False, extent).reshape(cell_rows, 27)
    pre_first = jnp.dot(first_taps, kernel_first, preferred_element_type=jnp.float32)
    hidden_first = jax.nn.silu(pre_first).astype(jnp.bfloat16)
    first_pad = close_rims(
        padded_2(
            hidden_first.reshape(slab_cells, rows_y, depth_cells, hidden),
            (("los", 0), ("tr", 1)),
            1,
        )
    )
    pre_second = second_conv(first_pad, kernel_second, extent, hidden)
    hidden_second = jax.nn.silu(pre_second).astype(jnp.bfloat16)
    second_pad = close_rims(
        padded_2(
            hidden_second.reshape(slab_cells, rows_y, depth_cells, hidden),
            (("los", 0), ("tr", 1)),
            1,
        )
    )
    projected = jnp.dot(
        second_pad.reshape(-1, hidden), third_matrix.T, preferred_element_type=jnp.float32
    )
    projected = projected.reshape(slab_cells + 2, rows_y + 2, depth_cells + 2, 27)
    log_rate = jnp.zeros(extent, jnp.float32)
    for tap_index in range(27):
        shift_x, shift_y, shift_z = (tap_index // 9, tap_index // 3 % 3, tap_index % 3)
        log_rate = (
            log_rate
            + projected[
                shift_x : shift_x + slab_cells,
                shift_y : shift_y + rows_y,
                shift_z : shift_z + depth_cells,
                tap_index,
            ]
        )
    rate_tiles = jnp.exp(log_rate).reshape(slab_cells, width_tiles, 128)
    targets = cell_targets.reshape(slab_cells, width_tiles, 128)
    line_index = jnp.arange(slab_cells, dtype=jnp.int32)[:, None]
    tile_index = jnp.arange(width_tiles, dtype=jnp.int32)[None, :]
    permuted = (
        jnp.zeros((slab_cells, width_tiles, 128), jnp.float32)
        .at[line_index[:, :, None], tile_index[:, :, None], targets]
        .add(rate_tiles)
    )
    reach_line = line_index + shift_bins
    block_step = jnp.floor_divide(reach_line, slab_cells)
    landing_line = reach_line - block_step * slab_cells
    landing_row = (landing_line * width_tiles + tile_index).reshape(-1)
    block_slot = (block_step + REACH).reshape(-1)
    flat_tiles = permuted.reshape(tile_total, 128)
    image_blocks = (
        jnp.zeros((spread, tile_total, 128), jnp.float32)
        .at[block_slot, landing_row]
        .add(flat_tiles)
    )
    arrived = image_blocks[REACH]
    for distance in range(-REACH, REACH + 1):
        if distance != 0:
            arrived = arrived + shifted(image_blocks[distance + REACH], "los", distance)
    redshift_rate = background + arrived
    counts = observed_counts.reshape(tile_total, 128).astype(jnp.float32)
    loss_part = jnp.sum(redshift_rate - counts * jnp.log(redshift_rate)) / total_cells
    lam_grad = (1.0 - counts / redshift_rate) / total_cells
    lam_blocks = lam_grad.reshape(slab_cells, width_tiles, 128)
    window_parts = []
    for distance in range(-REACH, REACH + 1):
        if distance == 0:
            window_parts.append(lam_blocks)
        else:
            window_parts.append(shifted(lam_blocks, "los", -distance))
    window = jnp.concatenate(window_parts, axis=0)
    permuted_grad = window[reach_line + REACH * slab_cells, tile_index]
    rate_grad = jnp.take_along_axis(permuted_grad, targets, axis=2)
    log_grad = (
        (rate_grad * rate_tiles).reshape(slab_cells, rows_y, depth_cells, 1).astype(jnp.bfloat16)
    )
    wide_log = jnp.pad(log_grad, ((2, 2), (2, 2), (2, 2), (0, 0)))
    wide_extent = (slab_cells + 2, rows_y + 2, depth_cells + 2)
    shifted_log = all_taps(wide_log, True, wide_extent).reshape(-1, 27)
    grad_third = contract_rows(second_pad.reshape(-1, hidden), shifted_log).T.reshape(
        27 * hidden, 1
    )
    log_pad = close_rims(padded_2(log_grad, (("los", 0), ("tr", 1)), 1))
    flipped_log = all_taps(log_pad, True, extent).reshape(cell_rows, 27)
    second_back = jnp.dot(flipped_log, third_matrix, preferred_element_type=jnp.float32)
    act_second = (second_back * silu_slope(pre_second)).astype(jnp.bfloat16)
    act_pad = close_rims(
        padded_2(
            act_second.reshape(slab_cells, rows_y, depth_cells, hidden), (("los", 0), ("tr", 1)), 1
        )
    )
    grad_blocks = []
    for shift_x in range(3):
        taps_block = plane_taps(first_pad, shift_x, False, extent).reshape(cell_rows, 9 * hidden)
        grad_blocks.append(contract_rows(taps_block, act_second))
    grad_second = jnp.concatenate(grad_blocks, axis=0)
    kernel_taps = kernel_second.reshape(3, 3, 3, hidden, hidden)
    first_back = jnp.zeros((cell_rows, hidden), jnp.float32)
    for shift_x in range(3):
        taps_block = plane_taps(act_pad, shift_x, True, extent).reshape(cell_rows, 9 * hidden)
        turned = kernel_taps[shift_x].transpose(0, 1, 3, 2).reshape(9 * hidden, hidden)
        first_back = first_back + jnp.dot(taps_block, turned, preferred_element_type=jnp.float32)
    act_first = (first_back * silu_slope(pre_first)).astype(jnp.bfloat16)
    grad_first = contract_rows(first_taps, act_first)
    grad_first, grad_second, grad_third, loss = lax.psum(
        (grad_first, grad_second, grad_third, loss_part), ("los", "tr")
    )
    return (
        redshift_rate.reshape(slab_cells, plane_cells),
        loss,
        grad_first,
        grad_second,
        grad_third,
    )


def solution(mesh):
    return jax.shard_map(
        on_device,
        mesh=mesh,
        in_specs=(P("los", "tr"), P("los", "tr"), P("los", "tr"), P("los", "tr"), P(), P(), P()),
        out_specs=(P("los", "tr"), P(), P(), P(), P()),
        check_vma=False,
    )
```

profile of v0, /device:TPU:0, one launch (start us, length us, event | category | flops | bytes accessed | tf_op | source)
XLA Modules:
  0.0 1030.4 jit_solution(4583347636332770826)
XLA Ops:
  8.7 5.1 collective-permute-start.1
  22.8 4.0 pad_slice_fusion.19
  26.8 4.0 pad_slice_fusion.18
  32.9 18.7 %concatenate.99 = bf16[16,24,48,27]{2,3,1,0:T(8,128)(2,1)S(1)} concatenate(bf16[16,24,48,1]{2,3,1,0:T(2,128)(2,1)} %get-tuple-element.239, bf16[16,24,48,1]{2,3,1,0:T(2,128)(2,1)} %get-tuple-element.238, bf16[16,24,48,1]{2,3,1,0:T(2,128)(2,1)} %get-tuple-element.214, bf16[16,24,48,1]{2,3,1,0:T(2,128)(2,1)} %get-tuple-element.215, bf16[16,24,48,1]{2,3,1,0:T(2,128)(2,1)} %get-tuple-element.237, ...), dimensions={3} | concatenate | bytes 1990656 | tf_op jit(solution)/shard_map/concatenate | solution.py:66
  54.2 6.3 reshape.617
  66.3 4.3 reshape.618
  71.0 4.5 collective-permute-start.5
  80.8 3.1 collective-permute-done.6
  99.6 2.9 slice_dynamic-update-slice_fusion.38
  102.5 3.9 slice_dynamic-update-slice_fusion.37
  106.5 4.4 slice_dynamic-update-slice_fusion.9
  110.9 13.8 %slice_dynamic-update-slice_fusion.36 = (bf16[16,24,48,288]{2,3,1,0:T(8,128)(2,1)}, bf16[16,24,48,288]{2,3,1,0:T(8,128)(2,1)}, bf16[16,24,48,288]{2,3,1,0:T(8,128)(2,1)}) fusion(bf16[16,24,48,288]{2,3,1,0:T(8,128)(2,1)} %get-tuple-element.156, bf16[18,26,48,32]{2,3,1,0:T(8,128)(2,1)S(1)} %fusion.20, bf16[16,24,48,288]{2,3,1,0:T(8,128)(2,1)} %get-tuple-element.157), kind=kLoop, calls=%fused_computation.59 | loop fusion | bytes 10874880 | tf_op jit(solution)/shard_map/concatenate | solution.py:62
  142.9 4.0 slice_dynamic-update-slice_fusion.42
  160.0 29.5 %copy.28 = bf16[16,24,48,288]{3,2,1,0:T(8,128)(2,1)} copy(bf16[16,24,48,288]{2,3,1,0:T(8,128)(2,1)} %slice_dynamic-update-slice_fusion.48) | data formatting | bytes 21233664 | tf_op jit(solution)/shard_map/concatenate | solution.py:62
  189.5 29.3 %copy.29 = bf16[16,24,48,288]{3,2,1,0:T(8,128)(2,1)} copy(bf16[16,24,48,288]{2,3,1,0:T(8,128)(2,1)} %get-tuple-element.160) | data formatting | bytes 21233664 | tf_op jit(solution)/shard_map/concatenate | solution.py:62
  218.7 29.3 %copy.30 = bf16[16,24,48,288]{3,2,1,0:T(8,128)(2,1)} copy(bf16[16,24,48,288]{2,3,1,0:T(8,128)(2,1)} %get-tuple-element.153) | data formatting | bytes 21233664 | tf_op jit(solution)/shard_map/concatenate | solution.py:62
  248.0 7.7 fusion.51
  257.1 4.4 convolution_add_fusion.3
  261.6 5.9 multiply_convert_fusion
  270.3 4.3 reshape.622
  274.9 4.5 collective-permute-start.9
  284.9 2.9 collective-permute-done.10
  295.7 3.0 copy-done.5
  298.8 6.9 slice_reduce_fusion.9
  307.5 14.5 %fusion.54 = (f32[16,24,48]{2,1,0:T(8,128)S(1)}, f32[16,24,48,1]{2,3,1,0:T(1,128)S(1)}) fusion(f32[]{:T(128)} %broadcast.432, f32[18,26,50,27]{2,3,1,0:T(8,128)} %copy-done.5), kind=kLoop, calls=%fused_computation.291 | loop fusion | flops 294912 | bytes 1400836 | tf_op jit(solution)/shard_map/add | solution.py:139
  322.3 127.3 %scatter_custom_fusion.1 = f32[18432]{0:T(1024)S(1)} fusion(s32[18432]{0:T(1024)S(1)} %reshape.663, f32[18432]{0:T(1024)S(1)} %reshape.665, f32[]{:T(128)} %constant.276.clone.1), kind=kCustom, calls=%fused_computation.186 | custom fusion | flops 18432 | bytes 73732
  449.7 7.7 scatter_fusion
  460.3 5.2 collective-permute-start.16
  465.4 4.9 collective-permute-start.17
  472.5 4.4 collective-permute-done.18
  481.6 4.6 collective-permute-done.22
  488.9 3.3 collective-permute-start.28
  493.5 5.6 collective-permute-done.24
  499.8 3.8 collective-permute-start.30
  506.2 3.3 collective-permute-start.35
  514.6 147.5 %gather_fusion.1 = f32[18432]{0:T(1024)S(1)} fusion(f32[16,9,128]{2,1,0:T(8,128)S(1)} %reshape.648, s32[18432]{0:T(1024)S(1)} %reshape.651), kind=kCustom, calls=%fused_computation.1 | custom fusion | bytes 368640 | tf_op jit(solution)/shard_map/jit(take_along_axis)/gather | solution.py:184
  662.6 9.6 fusion.17
  672.2 3.1 pad_slice_fusion.36
  675.3 3.9 pad_slice_fusion.37
  679.2 6.5 collective-permute-start.37
  685.8 4.1 pad_slice_fusion.38
  689.8 24.9 %concatenate.118 = bf16[18,26,50,27]{2,3,1,0:T(8,128)(2,1)} concatenate(bf16[18,26,50,1]{2,3,1,0:T(2,128)(2,1)} %get-tuple-element.270, bf16[18,26,50,1]{2,3,1,0:T(2,128)(2,1)S(1)} %get-tuple-element.245, bf16[18,26,50,1]{2,3,1,0:T(2,128)(2,1)S(1)} %get-tuple-element.246, bf16[18,26,50,1]{2,3,1,0:T(2,128)(2,1)S(1)} %get-tuple-element.247, ...), dimensions={3} | concatenate | bytes 2527200 | tf_op jit(solution)/shard_map/concatenate | solution.py:66
  716.8 6.5 fusion.13
  724.0 3.9 pad_slice_fusion.1
  728.0 4.0 pad_slice_fusion
  734.1 19.0 %concatenate.111 = bf16[16,24,48,27]{2,3,1,0:T(8,128)(2,1)S(1)} concatenate(bf16[16,24,48,1]{2,3,1,0:T(2,128)(2,1)} %get-tuple-element.212, bf16[16,24,48,1]{2,3,1,0:T(2,128)(2,1)} %get-tuple-element.211, bf16[16,24,48,1]{2,3,1,0:T(2,128)(2,1)} %get-tuple-element.187, bf16[16,24,48,1]{2,3,1,0:T(2,128)(2,1)} %get-tuple-element.188, bf16[16,24,48,1]{2,3,1,0:T(2,128)(2,1)} %get-tuple-element.210, ...), dimensions={3} | concatenate | bytes 1990656 | tf_op jit(solution)/shard_map/concatenate | solution.py:66
  755.6 6.3 reshape.628
  761.9 2.9 fusion
  764.9 7.0 fusion.67
  775.1 6.8 fusion.69
  781.8 4.2 reshape.629
  786.4 4.5 collective-permute-start.41
  791.8 4.1 copy_dynamic-update-slice_fusion
  822.8 4.0 slice_dynamic-update-slice_fusion.19
  826.7 4.4 slice_dynamic-update-slice_fusion
  831.1 5.6 slice_dynamic-update-slice_fusion.18
  854.9 4.0 slice_dynamic-update-slice_fusion.24
  872.1 29.6 %copy.52 = bf16[16,24,48,288]{3,2,1,0:T(8,128)(2,1)} copy(bf16[16,24,48,288]{2,3,1,0:T(8,128)(2,1)} %slice_dynamic-update-slice_fusion.30) | data formatting | bytes 21233664 | tf_op jit(solution)/shard_map/concatenate | solution.py:62
  901.6 29.3 %copy.54 = bf16[16,24,48,288]{3,2,1,0:T(8,128)(2,1)} copy(bf16[16,24,48,288]{2,3,1,0:T(8,128)(2,1)} %get-tuple-element.151) | data formatting | bytes 21233664 | tf_op jit(solution)/shard_map/concatenate | solution.py:62
  930.9 29.3 %copy.56 = bf16[16,24,48,288]{3,2,1,0:T(8,128)(2,1)} copy(bf16[16,24,48,288]{2,3,1,0:T(8,128)(2,1)} %get-tuple-element.144) | data formatting | bytes 21233664 | tf_op jit(solution)/shard_map/concatenate | solution.py:62
  960.3 7.7 fusion.66
  969.3 4.4 convolution_add_fusion.1
  973.8 8.7 fusion.3
  984.0 37.5 %all-reduce.6 = (f32[]{:T(128)}, f32[27,32]{1,0:T(8,128)}, f32[864,1]{0,1:T(1,128)}) all-reduce(f32[]{:T(128)S(6)} %div.39, f32[27,32]{1,0:T(8,128)} %fusion.3, f32[864,1]{0,1:T(1,128)S(1)} %reshape.636), channel_id=1, replica_groups=mesh['los'=16,'tr'=2] {'los','tr'}, use_global_device_ids=true, to_apply=%region_3.4 | all-reduce | flops 1729 | bytes 13832 | tf_op jit(solution)/shard_map/psum | solution.py:216
  (321 shorter events, 189.4 us)
Async XLA Ops:
  7.2 53.3 %copy-start = (bf16[27,32]{1,0:T(8,128)(2,1)S(1)}, bf16[27,32]{1,0:T(8,128)(2,1)}, u32[]{:S(2)}) copy-start(bf16[27,32]{1,0:T(8,128)(2,1)} %param.31) | copy-start | bytes 5188
  7.2 1014.4 %all-reduce.9.cloned.1.call-start = ((), (), s32[]{:S(2)}) async-start(), calls=%async_computation | async-start | bytes 229376 | tf_op jit(solution)/shard_map/psum | solution.py:216
  8.1 8.2 collective-permute-start
  8.7 7.9 collective-permute-start.1
  16.6 3.7 collective-permute-start.2
  18.6 3.7 collective-permute-start.3
  65.3 10.1 collective-permute-start.4
  71.0 7.7 collective-permute-start.5
  78.7 5.2 collective-permute-start.6
  78.9 6.6 collective-permute-start.7
  218.7 29.3 %copy-start.16 = (bf16[864,32]{0,1:T(8,128)(2,1)S(1)}, bf16[864,32]{0,1:T(8,128)(2,1)}, u32[]{:S(2)}) copy-start(bf16[864,32]{0,1:T(8,128)(2,1)} %param.32) | copy-start | bytes 165892
  248.0 13.5 %slice-start.4 = ((s8[14155776]{0:T(1024)(128)(4,1)}), s8[4194304]{0:T(1024)(128)(4,1)S(1)}, s32[]{:S(2)}) async-start(s8[14155776]{0:T(1024)(128)(4,1)} %bitcast.148), calls=%async_computation.5 | async-start | bytes 8388608
  248.0 13.5 %slice-start.5 = ((s8[14155776]{0:T(1024)(128)(4,1)}), s8[4194304]{0:T(1024)(128)(4,1)S(1)}, s32[]{:S(2)}) async-start(s8[14155776]{0:T(1024)(128)(4,1)} %bitcast.148), calls=%async_computation.6 | async-start | bytes 8388608
  269.5 9.9 collective-permute-start.8
  274.8 9.9 copy-start.28
  274.8 9.9 copy-start.29
  274.9 7.7 collective-permute-start.9
  282.6 5.2 collective-permute-start.10
  284.3 5.1 collective-permute-start.11
  322.0 148.3 %copy-start.17 = (bf16[864,32]{0,1:T(8,128)(2,1)S(1)}, bf16[864,32]{0,1:T(8,128)(2,1)}, u32[]{:S(2)}) copy-start(bf16[864,32]{0,1:T(8,128)(2,1)} %param.32) | copy-start | bytes 165892
  322.0 155.3 %copy-start.26 = (s32[16,9]{1,0:T(8,128)S(1)}, s32[16,9]{1,0:T(8,128)}, u32[]{:S(2)}) copy-start(s32[16,9]{1,0:T(8,128)} %param.30) | copy-start | bytes 1732
  322.0 155.3 %copy-start.14 = (s32[16,1152]{1,0:T(8,128)S(1)}, s32[16,1152]{1,0:T(8,128)}, u32[]{:S(2)}) copy-start(s32[16,1152]{1,0:T(8,128)} %param.29) | copy-start | bytes 221188
  322.1 156.4 %copy-start.24 = (s32[16,1152]{1,0:T(8,128)S(1)}, s32[16,1152]{1,0:T(8,128)}, u32[]{:S(2)}) copy-start(s32[16,1152]{1,0:T(8,128)} %param.28) | copy-start | bytes 221188
  322.1 156.5 %copy-start.12 = (s32[16,9,128,1]{2,1,0,3:T(8,128)S(1)}, s32[16,9,128,1]{2,1,0,3:T(8,128)}, u32[]{:S(2)}) copy-start(s32[16,9,128,1]{2,1,0,3:T(8,128)} %get-tuple-element.273) | copy-start | bytes 221188
  457.5 7.9 collective-permute-start.12
  457.6 12.8 %collective-permute-start.13 = (f32[144,128]{1,0:T(8,128)S(1)}, f32[144,128]{1,0:T(8,128)S(1)}, u32[]{:S(2)}, u32[]{:S(2)}) collective-permute-start(f32[144,128]{1,0:T(8,128)S(1)} %get-tuple-element.185), channel_id=1, source_target_pairs={{0,22},{2,24},{4,26},{6,28},{8,30},{10,0},{12,2},{14,4},{16,6},{18... | collective-permute-start | bytes 221192 | tf_op jit(solution)/shard_map/ppermute | solution.py:28
  458.2 12.2 %collective-permute-start.14 = (f32[144,128]{1,0:T(8,128)S(1)}, f32[144,128]{1,0:T(8,128)S(1)}, u32[]{:S(2)}, u32[]{:S(2)}) collective-permute-start(f32[144,128]{1,0:T(8,128)S(1)} %get-tuple-element.184), channel_id=1, source_target_pairs={{0,24},{2,26},{4,28},{6,30},{8,0},{10,2},{12,4},{14,6},{16,8},{18,... | collective-permute-start | bytes 221192 | tf_op jit(solution)/shard_map/ppermute | solution.py:28
  460.1 10.5 %collective-permute-start.15 = (f32[144,128]{1,0:T(8,128)S(1)}, f32[144,128]{1,0:T(8,128)S(1)}, u32[]{:S(2)}, u32[]{:S(2)}) collective-permute-start(f32[144,128]{1,0:T(8,128)S(1)} %get-tuple-element.183), channel_id=1, source_target_pairs={{0,26},{2,28},{4,30},{6,0},{8,2},{10,4},{12,6},{14,8},{16,10},{18,... | collective-permute-start | bytes 221192 | tf_op jit(solution)/shard_map/ppermute | solution.py:28
  460.3 10.4 %collective-permute-start.16 = (f32[144,128]{1,0:T(8,128)S(1)}, f32[144,128]{1,0:T(8,128)S(1)}, u32[]{:S(2)}, u32[]{:S(2)}) collective-permute-start(f32[144,128]{1,0:T(8,128)S(1)} %get-tuple-element.182), channel_id=1, source_target_pairs={{0,28},{2,30},{4,0},{6,2},{8,4},{10,6},{12,8},{14,10},{16,12},{18,... | collective-permute-start | bytes 221192 | tf_op jit(solution)/shard_map/ppermute | solution.py:28
  465.4 7.1 collective-permute-start.17
  470.4 6.6 collective-permute-start.18
  470.5 11.1 %collective-permute-start.19 = (f32[144,128]{1,0:T(8,128)S(1)}, f32[144,128]{1,0:T(8,128)S(1)}, u32[]{:S(2)}, u32[]{:S(2)}) collective-permute-start(f32[144,128]{1,0:T(8,128)S(1)} %get-tuple-element.179), channel_id=1, source_target_pairs={{0,4},{2,6},{4,8},{6,10},{8,12},{10,14},{12,16},{14,18},{16,20},{1... | collective-permute-start | bytes 221192 | tf_op jit(solution)/shard_map/ppermute | solution.py:28
  470.5 11.0 %collective-permute-start.20 = (f32[144,128]{1,0:T(8,128)S(1)}, f32[144,128]{1,0:T(8,128)S(1)}, u32[]{:S(2)}, u32[]{:S(2)}) collective-permute-start(f32[144,128]{1,0:T(8,128)S(1)} %get-tuple-element.178), channel_id=1, source_target_pairs={{0,6},{2,8},{4,10},{6,12},{8,14},{10,16},{12,18},{14,20},{16,22},{... | collective-permute-start | bytes 221192 | tf_op jit(solution)/shard_map/ppermute | solution.py:28
  470.6 10.9 %collective-permute-start.21 = (f32[144,128]{1,0:T(8,128)S(1)}, f32[144,128]{1,0:T(8,128)S(1)}, u32[]{:S(2)}, u32[]{:S(2)}) collective-permute-start(f32[144,128]{1,0:T(8,128)S(1)} %get-tuple-element.177), channel_id=1, source_target_pairs={{0,8},{2,10},{4,12},{6,14},{8,16},{10,18},{12,20},{14,22},{16,24},... | collective-permute-start | bytes 221192 | tf_op jit(solution)/shard_map/ppermute | solution.py:28
  472.5 13.7 %collective-permute-start.22 = (f32[144,128]{1,0:T(8,128)S(1)}, f32[144,128]{1,0:T(8,128)S(1)}, u32[]{:S(2)}, u32[]{:S(2)}) collective-permute-start(f32[144,128]{1,0:T(8,128)S(1)} %get-tuple-element.176), channel_id=1, source_target_pairs={{0,10},{2,12},{4,14},{6,16},{8,18},{10,20},{12,22},{14,24},{16,26}... | collective-permute-start | bytes 221192 | tf_op jit(solution)/shard_map/ppermute | solution.py:28
  476.9 9.5 collective-permute-start.23
  486.5 175.7 %copy-start.11 = (f32[144,128]{1,0:T(8,128)}, f32[144,128]{1,0:T(8,128)S(1)}, u32[]{:S(2)}) copy-start(f32[144,128]{1,0:T(8,128)S(1)} %get-tuple-element.141) | copy-start | bytes 221188
  486.6 12.5 %collective-permute-start.24 = (f32[16,9,128]{2,0,1:T(8,128)S(1)}, f32[16,9,128]{2,0,1:T(8,128)S(1)}, u32[]{:S(2)}, u32[]{:S(2)}) collective-permute-start(f32[16,9,128]{2,0,1:T(8,128)S(1)} %copy.35), channel_id=1, source_target_pairs={{0,12},{2,14},{4,16},{6,18},{8,20},{10,22},{12,24},{14,26},{16,28}... | collective-permute-start | bytes 221192 | tf_op jit(solution)/shard_map/ppermute | solution.py:28
  486.6 13.2 %collective-permute-start.25 = (f32[16,9,128]{2,0,1:T(8,128)S(1)}, f32[16,9,128]{2,0,1:T(8,128)S(1)}, u32[]{:S(2)}, u32[]{:S(2)}) collective-permute-start(f32[16,9,128]{2,0,1:T(8,128)S(1)} %copy.35), channel_id=1, source_target_pairs={{0,10},{2,12},{4,14},{6,16},{8,18},{10,20},{12,22},{14,24},{16,26}... | collective-permute-start | bytes 221192 | tf_op jit(solution)/shard_map/ppermute | solution.py:28
  486.9 16.7 %collective-permute-start.26 = (f32[16,9,128]{2,0,1:T(8,128)S(1)}, f32[16,9,128]{2,0,1:T(8,128)S(1)}, u32[]{:S(2)}, u32[]{:S(2)}) collective-permute-start(f32[16,9,128]{2,0,1:T(8,128)S(1)} %copy.35), channel_id=1, source_target_pairs={{0,8},{2,10},{4,12},{6,14},{8,16},{10,18},{12,20},{14,22},{16,24},... | collective-permute-start | bytes 221192 | tf_op jit(solution)/shard_map/ppermute | solution.py:28
  486.9 16.8 %collective-permute-start.27 = (f32[16,9,128]{2,0,1:T(8,128)S(1)}, f32[16,9,128]{2,0,1:T(8,128)S(1)}, u32[]{:S(2)}, u32[]{:S(2)}) collective-permute-start(f32[16,9,128]{2,0,1:T(8,128)S(1)} %copy.35), channel_id=1, source_target_pairs={{0,6},{2,8},{4,10},{6,12},{8,14},{10,16},{12,18},{14,20},{16,22},{... | collective-permute-start | bytes 221192 | tf_op jit(solution)/shard_map/ppermute | solution.py:28
  488.9 14.9 %collective-permute-start.28 = (f32[16,9,128]{2,0,1:T(8,128)S(1)}, f32[16,9,128]{2,0,1:T(8,128)S(1)}, u32[]{:S(2)}, u32[]{:S(2)}) collective-permute-start(f32[16,9,128]{2,0,1:T(8,128)S(1)} %copy.35), channel_id=1, source_target_pairs={{0,4},{2,6},{4,8},{6,10},{8,12},{10,14},{12,16},{14,18},{16,20},{1... | collective-permute-start | bytes 221192 | tf_op jit(solution)/shard_map/ppermute | solution.py:28
  499.0 7.1 collective-permute-start.29
  499.8 6.4 collective-permute-start.30
  503.6 6.0 collective-permute-start.31
  503.6 5.9 collective-permute-start.32
  503.7 7.2 collective-permute-start.33
  506.1 6.0 collective-permute-start.34
  506.2 6.7 collective-permute-start.35
  679.2 35.5 %collective-permute-start.36 = (bf16[1,24,48,1]{2,3,1,0:T(2,128)(2,1)S(1)}, bf16[1,24,48,1]{2,3,1,0:T(2,128)(2,1)S(1)}, u32[]{:S(2)}, u32[]{:S(2)}) collective-permute-start(bf16[1,24,48,1]{2,3,1,0:T(2,128)(2,1)S(1)} %get-tuple-element.271), channel_id=1, source_target_pairs={{0,2},{2,4},{4,6},{6,8},{8,10},{10,12},{12,14},{14,16},{16,18},{18... | collective-permute-start | bytes 6920 | tf_op jit(solution)/shard_map/ppermute | solution.py:20
  679.2 35.5 %collective-permute-start.37 = (bf16[1,24,48,1]{2,3,1,0:T(2,128)(2,1)S(1)}, bf16[1,24,48,1]{2,3,1,0:T(2,128)(2,1)S(1)}, u32[]{:S(2)}, u32[]{:S(2)}) collective-permute-start(bf16[1,24,48,1]{2,3,1,0:T(2,128)(2,1)S(1)} %get-tuple-element.272), channel_id=1, source_target_pairs={{2,0},{4,2},{6,4},{8,6},{10,8},{12,10},{14,12},{16,14},{18,16},{20... | collective-permute-start | bytes 6920 | tf_op jit(solution)/shard_map/ppermute | solution.py:21
  714.7 8.7 collective-permute-start.38
  715.2 8.2 collective-permute-start.39
  761.9 9.9 slice-start
  761.9 9.9 slice-start.1
  775.0 15.8 %collective-permute-start.40 = (bf16[1,24,48,32]{2,3,1,0:T(8,128)(2,1)S(1)}, bf16[1,24,48,32]{2,3,1,0:T(8,128)(2,1)}, u32[]{:S(2)}, u32[]{:S(2)}) collective-permute-start(bf16[1,24,48,32]{2,3,1,0:T(8,128)(2,1)S(1)} %copy.49), channel_id=1, source_target_pairs={{0,2},{2,4},{4,6},{6,8},{8,10},{10,12},{12,14},{14,16},{16,18},{18... | collective-permute-start | bytes 221192 | tf_op jit(solution)/shard_map/ppermute | solution.py:20
  786.3 12.4 %copy-start.18 = (f32[288,32]{0,1:T(8,128)S(1)}, f32[288,32]{0,1:T(8,128)}, u32[]{:S(2)}) copy-start(f32[288,32]{0,1:T(8,128)} %fusion.67) | copy-start | bytes 110596
  786.3 12.4 %copy-start.19 = (f32[288,32]{0,1:T(8,128)S(1)}, f32[288,32]{0,1:T(8,128)}, u32[]{:S(2)}) copy-start(f32[288,32]{0,1:T(8,128)} %fusion.68) | copy-start | bytes 110596
  786.3 12.4 %copy-start.20 = (f32[288,32]{0,1:T(8,128)S(1)}, f32[288,32]{0,1:T(8,128)}, u32[]{:S(2)}) copy-start(f32[288,32]{0,1:T(8,128)} %fusion.69) | copy-start | bytes 110596
  786.4 9.5 collective-permute-start.41
  796.7 5.5 collective-permute-start.42
  797.2 6.6 collective-permute-start.43
  930.9 29.3 %copy-start.22 = (bf16[288,32]{0,1:T(8,128)(2,1)S(1)}, bf16[288,32]{0,1:T(8,128)(2,1)}, u32[]{:S(2)}) copy-start(bf16[288,32]{0,1:T(8,128)(2,1)} %reshape.631) | copy-start | bytes 55300
  973.8 49.3 %copy-start.1 = (bf16[27,32]{1,0:T(8,128)(2,1)S(1)}, bf16[27,32]{1,0:T(8,128)(2,1)}, u32[]{:S(2)}) copy-start(bf16[27,32]{1,0:T(8,128)(2,1)} %param.31) | copy-start | bytes 5188
  (20 other events, 111.4 us)
Sparse Core Ops, SparseCore 0:
  799.6 118.6 all-reduce.8
where the time goes:
time: 1050 us; the launch traced here: 1030 us
  local copies, waits for them, and re-layouts  636 us (61%)
  other arithmetic  172 us (16%)
  matrix products  68.4 us (7%)
  starting transfers between devices  61.4 us (6%)
  waiting for transfers between devices  38.6 us (4%)
  blocking collectives  37.5 us (4%)
  between operations  16.5 us (2%)
    concatenate x12, local copies, waits for them, and re-layouts, plane_taps(): return jnp.concatenate(pieces, axis=-1)  209 us
    gather x2, local copies, waits for them, and re-layouts, on_device(): rate_grad = jnp.take_along_axis(permuted_grad, targets, axis=2)  148 us
    unnamed x138, local copies, waits for them, and re-layouts  130 us
    unnamed x7, other arithmetic  129 us
    concatenate x5, local copies, waits for them, and re-layouts, all_taps(): jnp.concatenate([plane_taps(padded, shift_x, flipped, extent) for shift_x...  67.6 us
    psum x1, blocking collectives, on_device(): lax.psum((grad_first, grad_second, grad_third, loss_part), ('los', 'tr'))  37.5 us
    dot_general x5, matrix products, contract_rows(): lax.dot_general(left, right, (((0,), (0,)), ((), ())), preferred_element_...  31.8 us
    slice x9, local copies, waits for them, and re-layouts, plane_taps(): padded[anchor[0]:anchor[0] + extent[0], anchor[1]:anchor[1] + extent[1],...  31.4 us
  transfers between devices with their start and end apart: 45, of which 18 were waited for; matrix products, arithmetic and copies ran while one was open for 25% of the time, Pallas kernels for 0%

commit v1 on v0

v1 whole, which is shorter than its diff:
```python
import functools

import jax
import jax.numpy as jnp
from jax import lax
from jax.experimental import pallas as pl
from jax.experimental.pallas import tpu as pltpu
from jax.sharding import PartitionSpec as P

NZ = 48
REACH = 6
SPREAD = 2 * REACH + 1
CAP = 24
PITCH = 32
SLOTS = SPREAD * PITCH
HID = 32
YP = 32
OFF = 4
LANES = NZ * HID
PAD = 128
WIDE = LANES + 2 * PAD
GROUP = 256
GROUPS = LANES // GROUP
BACKGROUND = 0.2
MESH = pl.DeviceIdType.MESH
HIGH = lax.Precision.HIGHEST
LIMIT = 56 * 1024 * 1024
F32 = jnp.float32
BF16 = jnp.bfloat16
NT = (((1,), (1,)), ((), ()))
TN = (((0,), (0,)), ((), ()))


def iota(shape, dim):
    return lax.broadcasted_iota(jnp.int32, shape, dim)


def repeat_lanes(kernel, width):
    rep = jnp.where((iota((HID, width), 1) & (HID - 1)) == iota((HID, width), 0), 1.0, 0.0)
    return jnp.dot(kernel, rep.astype(BF16), preferred_element_type=F32)


def fill_thin_band(kernel, out_ref, flip):
    tiled = repeat_lanes(kernel, LANES)
    diff = iota((NZ, LANES), 0) - (iota((NZ, LANES), 1) >> 5)
    if flip:
        diff = -diff
    for ab in range(9):
        block = jnp.zeros((NZ, LANES), F32)
        for c in range(3):
            row = 3 * ab + c
            block = jnp.where(diff == c - 1, tiled[row : row + 1, :], block)
        out_ref[ab * NZ : (ab + 1) * NZ, :] = block.astype(BF16)


def fill_wide_band(kernel, out_ref):
    tiled = repeat_lanes(kernel, GROUP)
    zo = iota((HID, GROUP), 1) >> 5
    for ab in range(9):
        for zi in range(16):
            block = jnp.zeros((HID, GROUP), F32)
            for c in range(3):
                if 0 <= zi - 3 - c < 8:
                    row = (3 * ab + c) * HID
                    block = jnp.where(zo == zi - 3 - c, tiled[row : row + HID, :], block)
            out_ref[ab, zi * HID : (zi + 1) * HID, :] = block.astype(BF16)


def fill_taps(src_ref, out_ref, lines):
    for ab in range(9):
        a, b = ab // 3, ab % 3
        out_ref[:, :, ab * NZ : (ab + 1) * NZ] = src_ref[a : a + lines, b : b + YP, :]


def y_masks(rows_y, lines, width):
    index = iota((lines, YP, width), 1) - OFF
    start = lax.axis_index("tr") * rows_y
    total = lax.axis_size("tr") * rows_y
    inside = (index + start >= 0) & (index + start < total)
    owned = (index >= 0) & (index < rows_y)
    return inside, owned


def sigmoid(v):
    return 1.0 / (1.0 + jnp.exp(-v))


def slope(v):
    s = sigmoid(v)
    return s * (1.0 + v * (1.0 - s))


def store_shifted(out_ref, g, value):
    lanes = pl.ds(pl.multiple_of(PAD + g * GROUP, 128), GROUP)
    out_ref[0, :, :, lanes] = pltpu.roll(value, 1, 1).astype(BF16)
    out_ref[1, :, :, lanes] = value.astype(BF16)
    out_ref[2, :, :, lanes] = pltpu.roll(value, YP - 1, 1).astype(BF16)


def clear_pads(out_ref):
    shape = out_ref.shape[:-1] + (PAD,)
    out_ref[:, :, :, 0:PAD] = jnp.zeros(shape, BF16)
    out_ref[:, :, :, WIDE - PAD : WIDE] = jnp.zeros(shape, BF16)


def wide_conv(src_ref, band_ref, g, lines):
    total = jnp.zeros((lines * YP, GROUP), F32)
    lanes = pl.ds(pl.multiple_of(g * GROUP, 128), 2 * GROUP)
    for ab in range(9):
        a, b = ab // 3, ab % 3
        block = src_ref[b, a : a + lines, :, lanes].reshape(lines * YP, 2 * GROUP)
        total = total + jnp.dot(block, band_ref[ab], preferred_element_type=F32)
    return total


def forward_kernel(
    lines, rows_y, field_ref, k1_ref, k2_ref, k3_ref,
    rate_ref, pre1_ref, pre2_ref, h1_ref, h2_ref, taps_ref,
    d9, w1, w2, w3, h1b, h2, z9,
):
    l2, l1 = lines + 4, lines + 2
    fill_thin_band(k1_ref[...], w1, False)
    fill_wide_band(k2_ref[...], w2)
    fill_thin_band(k3_ref[...], w3, True)
    fill_taps(field_ref, d9, l2)
    taps_ref[...] = d9[2 : 2 + lines].reshape(lines * YP, 9 * NZ).astype(BF16)
    clear_pads(h1b)

    @pl.loop(0, GROUPS)
    def _(g):
        lanes = pl.ds(pl.multiple_of(g * GROUP, 128), GROUP)
        taps = d9[...].reshape(l2 * YP, 9 * NZ).astype(BF16)
        pre = jnp.dot(taps, w1[:, lanes], preferred_element_type=F32)
        pre = pre.reshape(l2, YP, GROUP)
        pre1_ref[:, :, lanes] = pre[2 : 2 + lines]
        inside, _ = y_masks(rows_y, l2, GROUP)
        _, owned = y_masks(rows_y, lines, GROUP)
        value = jnp.where(inside, pre * sigmoid(pre), 0.0)
        h1_ref[:, :, lanes] = jnp.where(owned, value[2 : 2 + lines], 0.0).astype(BF16)
        store_shifted(h1b, g, value)

    @pl.loop(0, GROUPS)
    def _(g):
        lanes = pl.ds(pl.multiple_of(g * GROUP, 128), GROUP)
        pre = wide_conv(h1b, w2, g, l1).reshape(l1, YP, GROUP)
        pre2_ref[:, :, lanes] = pre
        inside, _ = y_masks(rows_y, l1, GROUP)
        _, owned = y_masks(rows_y, lines, GROUP)
        value = jnp.where(inside, pre * sigmoid(pre), 0.0)
        h2[:, :, lanes] = value.astype(BF16)
        h2_ref[:, :, lanes] = jnp.where(owned, value[1 : 1 + lines], 0.0).astype(BF16)

    z9[...] = lax.dot_general(
        h2[...].reshape(l1 * YP, LANES), w3[...], NT, preferred_element_type=F32
    ).reshape(l1, YP, 9 * NZ)
    total = jnp.zeros((lines, rows_y, NZ), F32)
    for ab in range(9):
        a, b = ab // 3, ab % 3
        row = OFF - 1 + b
        total = total + z9[a : a + lines, row : row + rows_y, ab * NZ : (ab + 1) * NZ]
    rate_ref[...] = jnp.exp(total)


def tile_kernel(
    total_cells, rate_ref, target_ref, count_ref, slot_ref, land_ref,
    red_ref, loss_ref, grad_ref,
    msg, recv, back, ret, marks, send_sem, recv_sem, send_back, recv_back,
):
    tiles = rate_ref.shape[0]
    me, other = lax.axis_index("los"), lax.axis_index("tr")
    size = lax.axis_size("los")

    def peer(distance):
        return (lax.rem(me + distance + size, size), other)

    distances = [d for d in range(SPREAD) if d != REACH]
    barrier = pltpu.get_barrier_semaphore()
    for d in distances:
        pl.semaphore_signal(barrier, inc=1, device_id=peer(d - REACH), device_id_type=MESH)

    def add_tile(t, perm):
        hit = iota((128, 128), 0) == target_ref[pl.ds(t, 1), :]
        column = jnp.sum(jnp.where(hit, rate_ref[pl.ds(t, 1), :], 0.0), axis=1, keepdims=True)
        return jnp.where(iota((128, tiles), 1) == t, column, perm)

    perm = lax.fori_loop(0, tiles, add_tile, jnp.zeros((128, tiles), F32), unroll=4)
    pick = jnp.where(iota((SLOTS, tiles), 0) == slot_ref[...], 1.0, 0.0)
    sent = lax.dot_general(pick, perm, NT, precision=HIGH, preferred_element_type=F32)
    sent = sent.reshape(SPREAD, PITCH, 128)
    landing = land_ref[...].reshape(SPREAD, 1, 128)
    msg[...] = jnp.where(iota((SPREAD, PITCH, 128), 1) == CAP, landing, sent)

    pl.semaphore_wait(barrier, len(distances))
    copies = []
    for d in distances:
        copy = pltpu.make_async_remote_copy(
            src_ref=msg.at[d], dst_ref=recv.at[d],
            send_sem=send_sem.at[d], recv_sem=recv_sem.at[d],
            device_id=peer(d - REACH), device_id_type=MESH,
        )
        copy.start()
        copies.append(copy)
    recv[REACH] = msg[REACH]
    for copy in copies:
        copy.wait_recv()
    for d in range(SPREAD):
        marks[0:1, d * PITCH : (d + 1) * PITCH] = recv[d, CAP : CAP + 1, 0:PITCH]
    place = jnp.where(
        iota((tiles, SLOTS), 0).astype(F32) == marks[0:1, 0:SLOTS], 1.0, 0.0
    )
    arrived = jnp.dot(
        place, recv[...].reshape(SLOTS, 128), precision=HIGH, preferred_element_type=F32
    )
    rate = BACKGROUND + arrived
    red_ref[...] = rate
    counts = count_ref[...].astype(F32)
    lam = (1.0 - counts / rate) / total_cells
    back[...] = lax.dot_general(
        place, lam, TN, precision=HIGH, preferred_element_type=F32
    ).reshape(SPREAD, PITCH, 128)
    returns = []
    for d in distances:
        copy = pltpu.make_async_remote_copy(
            src_ref=back.at[d], dst_ref=ret.at[d],
            send_sem=send_back.at[d], recv_sem=recv_back.at[d],
            device_id=peer(REACH - d), device_id_type=MESH,
        )
        copy.start()
        returns.append(copy)
    ret[REACH] = back[REACH]
    loss_ref[...] = jnp.sum(rate - counts * jnp.log(rate), axis=0, keepdims=True) / total_cells
    for copy in returns:
        copy.wait_recv()
    moved = lax.dot_general(
        pick, ret[...].reshape(SLOTS, 128), TN, precision=HIGH, preferred_element_type=F32
    )
    picked = jnp.take_along_axis(moved, target_ref[...], axis=1)
    grad_ref[...] = (picked * rate_ref[...]).astype(BF16)
    for copy in copies + returns:
        copy.wait_send()


def thin_extract(product, fold):
    diff = iota((NZ, LANES), 0) - (iota((NZ, LANES), 1) >> 5)
    rows = []
    for ab in range(9):
        block = product[ab * NZ : (ab + 1) * NZ, :]
        for c in range(3):
            rows.append(
                jnp.sum(jnp.where(diff == c - 1, block, 0.0), axis=0, keepdims=True)
            )
    rows = jnp.concatenate(rows + [jnp.zeros((5, LANES), F32)], axis=0)
    return jnp.dot(rows, fold, precision=HIGH, preferred_element_type=F32)


def fold_matrix(width):
    return jnp.where((iota((width, HID), 0) & (HID - 1)) == iota((width, HID), 1), 1.0, 0.0)


def backward_kernel(
    lines, rows_y, grad_ref, pre1_ref, pre2_ref, h1_ref, h2_ref, taps_ref, k2_ref, k3_ref,
    out_ref,
    g9, w2, w3, a2b, a1, h1t, prod, sums,
):
    l1 = lines + 2
    fill_wide_band(k2_ref[...], w2)
    fill_thin_band(k3_ref[...], w3, False)
    fill_taps(grad_ref, g9, l1)
    clear_pads(a2b)

    @pl.loop(0, GROUPS)
    def _(g):
        lanes = pl.ds(pl.multiple_of(g * GROUP, 128), GROUP)
        taps = g9[...].reshape(l1 * YP, 9 * NZ).astype(BF16)
        grad = jnp.dot(taps, w3[:, lanes], preferred_element_type=F32)
        grad = grad.reshape(l1, YP, GROUP) * slope(pre2_ref[:, :, lanes])
        inside, _ = y_masks(rows_y, l1, GROUP)
        store_shifted(a2b, g, jnp.where(inside, grad, 0.0))
        h1t[g] = h1_ref[:, :, lanes].reshape(lines * YP, GROUP).astype(F32).T.astype(BF16)

    @pl.loop(0, GROUPS)
    def _(g):
        lanes = pl.ds(pl.multiple_of(g * GROUP, 128), GROUP)
        grad = wide_conv(a2b, w2, g, lines).reshape(lines, YP, GROUP)
        grad = grad * slope(pre1_ref[:, :, lanes])
        _, owned = y_masks(rows_y, lines, GROUP)
        a1[:, :, lanes] = jnp.where(owned, grad, 0.0).astype(BF16)

    fold = fold_matrix(LANES)
    prod[...] = lax.dot_general(
        taps_ref[...], a1[...].reshape(lines * YP, LANES), TN, preferred_element_type=F32
    )
    out_ref[27 * HID : 28 * HID, :] = thin_extract(prod, fold)
    prod[...] = lax.dot_general(
        g9[1 : 1 + lines].reshape(lines * YP, 9 * NZ).astype(BF16),
        h2_ref[...].reshape(lines * YP, LANES), TN, preferred_element_type=F32,
    )
    out_ref[28 * HID : 29 * HID, :] = thin_extract(prod, fold)

    lane_z = iota((HID, 2 * GROUP), 1) >> 5
    for ab in range(9):
        a, b = ab // 3, ab % 3
        total = jnp.zeros((GROUP, 2 * GROUP), F32)
        for g in range(GROUPS):
            block = a2b[b, a : a + lines, :, g * GROUP : (g + 2) * GROUP]
            total = total + jnp.dot(
                h1t[g], block.reshape(lines * YP, 2 * GROUP), preferred_element_type=F32
            )
        for c in range(3):
            part = jnp.zeros((HID, 2 * GROUP), F32)
            for z in range(8):
                part = jnp.where(lane_z == z + 3 + c, total[z * HID : (z + 1) * HID, :], part)
            row = (26 - 3 * ab - c) * HID
            sums[row : row + HID, :] = part
    out_ref[0 : 27 * HID, :] = jnp.dot(
        sums[...], fold_matrix(2 * GROUP), precision=HIGH, preferred_element_type=F32
    )


def extended(block, width):
    lines, rows, depth = block.shape
    position = lax.axis_index("tr")
    size = lax.axis_size("los")
    send = jnp.where(position == 0, block[:, rows - width :], block[:, :width])
    got = lax.ppermute(send, "tr", [(0, 1), (1, 0)])
    none = jnp.zeros_like(got)
    gap = OFF + 1 - width
    low = jnp.where(position == 1, got, none)
    high = jnp.where(position == 0, got, none)
    wide = jnp.concatenate([low, block, high], axis=1)
    wide = jnp.pad(wide, ((0, 0), (gap, YP + 2 - gap - rows - 2 * width), (0, 0)))
    up = [(i, (i + 1) % size) for i in range(size)]
    down = [(j, i) for i, j in up]
    before = lax.ppermute(wide[lines - width :], "los", up)
    after = lax.ppermute(wide[:width], "los", down)
    return jnp.concatenate([before, wide, after], axis=0).astype(F32)


def on_device(
    density, observed_counts, cell_targets, shift_bins, kernel_first, kernel_second, kernel_third
):
    lines, width_tiles = shift_bins.shape
    plane = density.shape[1]
    rows_y = plane // NZ
    tiles = lines * width_tiles
    total_cells = lines * lax.axis_size("los") * plane * lax.axis_size("tr")
    l1, l2 = lines + 2, lines + 4
    vmem = pl.BlockSpec(memory_space=pltpu.VMEM)
    third = kernel_third.reshape(27, HID)
    second_back = kernel_second.reshape(27, HID, HID)[::-1].transpose(0, 2, 1).reshape(-1, HID)

    line = jnp.arange(lines, dtype=jnp.int32)[:, None]
    tile = jnp.arange(width_tiles, dtype=jnp.int32)[None, :]
    reach_line = line + shift_bins
    step = jnp.floor_divide(reach_line, lines)
    landing = ((reach_line - step * lines) * width_tiles + tile).reshape(-1)
    step = (step + REACH).reshape(-1)
    order = jnp.arange(tiles)
    earlier = (step[:, None] == step[None, :]) & (order[:, None] < order[None, :])
    rank = jnp.sum(earlier.astype(jnp.int32), axis=0)
    slot = step * PITCH + rank
    marks = jnp.sum(
        jnp.where(slot[:, None] == jnp.arange(SLOTS)[None, :], landing[:, None] + 1, 0), axis=0
    ) - 1
    marks = jnp.pad(
        marks.astype(F32).reshape(SPREAD, PITCH), ((0, 0), (0, 128 - PITCH)), constant_values=-1.0
    )

    field = extended(density.reshape(lines, rows_y, NZ), 3)
    rate, pre1, pre2, h1, h2, taps = pl.pallas_call(
        functools.partial(forward_kernel, lines, rows_y),
        out_shape=[
            jax.ShapeDtypeStruct((lines, rows_y, NZ), F32),
            jax.ShapeDtypeStruct((lines, YP, LANES), F32),
            jax.ShapeDtypeStruct((l1, YP, LANES), F32),
            jax.ShapeDtypeStruct((lines, YP, LANES), BF16),
            jax.ShapeDtypeStruct((lines, YP, LANES), BF16),
            jax.ShapeDtypeStruct((lines * YP, 9 * NZ), BF16),
        ],
        in_specs=[vmem] * 4,
        out_specs=[vmem] * 6,
        scratch_shapes=[
            pltpu.VMEM((l2, YP, 9 * NZ), F32),
            pltpu.VMEM((9 * NZ, LANES), BF16),
            pltpu.VMEM((9, 2 * GROUP, GROUP), BF16),
            pltpu.VMEM((9 * NZ, LANES), BF16),
            pltpu.VMEM((3, l2, YP, WIDE), BF16),
            pltpu.VMEM((l1, YP, LANES), BF16),
            pltpu.VMEM((l1, YP, 9 * NZ), F32),
        ],
        compiler_params=pltpu.CompilerParams(vmem_limit_bytes=LIMIT),
        name="forward",
    )(field, kernel_first, kernel_second, third)

    box = pltpu.VMEM((SPREAD, PITCH, 128), F32)
    sems = pltpu.SemaphoreType.DMA((SPREAD,))
    redshift_rate, loss_part, log_grad = pl.pallas_call(
        functools.partial(tile_kernel, total_cells),
        out_shape=[
            jax.ShapeDtypeStruct((tiles, 128), F32),
            jax.ShapeDtypeStruct((1, 128), F32),
            jax.ShapeDtypeStruct((tiles, 128), BF16),
        ],
        in_specs=[vmem] * 5,
        out_specs=[vmem] * 3,
        scratch_shapes=[box, box, box, box, pltpu.VMEM((8, 512), F32), sems, sems, sems, sems],
        compiler_params=pltpu.CompilerParams(
            vmem_limit_bytes=LIMIT, collective_id=0, has_side_effects=True
        ),
        name="tiles",
    )(
        rate.reshape(tiles, 128),
        cell_targets.reshape(tiles, 128),
        observed_counts.reshape(tiles, 128),
        slot.reshape(1, tiles),
        marks,
    )

    grad = extended(log_grad.reshape(lines, rows_y, NZ), 2)
    packed = pl.pallas_call(
        functools.partial(backward_kernel, lines, rows_y),
        out_shape=jax.ShapeDtypeStruct((29 * HID, HID), F32),
        in_specs=[vmem] * 8,
        out_specs=vmem,
        scratch_shapes=[
            pltpu.VMEM((l1, YP, 9 * NZ), F32),
            pltpu.VMEM((9, 2 * GROUP, GROUP), BF16),
            pltpu.VMEM((9 * NZ, LANES), BF16),
            pltpu.VMEM((3, l1, YP, WIDE), BF16),
            pltpu.VMEM((lines, YP, LANES), BF16),
            pltpu.VMEM((GROUPS, GROUP, lines * YP), BF16),
            pltpu.VMEM((9 * NZ, LANES), F32),
            pltpu.VMEM((27 * HID, 2 * GROUP), F32),
        ],
        compiler_params=pltpu.CompilerParams(vmem_limit_bytes=LIMIT),
        name="backward",
    )(grad, pre1, pre2, h1, h2, taps, second_back, third[::-1])
    packed = packed.at[29 * HID - 1, 0].set(jnp.sum(loss_part))
    packed = lax.psum(packed, ("los", "tr"))
    return (
        redshift_rate.reshape(lines, plane),
        packed[29 * HID - 1, 0],
        packed[27 * HID : 27 * HID + 27],
        packed[: 27 * HID],
        packed[28 * HID : 28 * HID + 27][::-1].reshape(27 * HID, 1),
    )


def solution(mesh):
    return jax.shard_map(
        on_device,
        mesh=mesh,
        in_specs=(P("los", "tr"), P("los", "tr"), P("los", "tr"), P("los", "tr"), P(), P(), P()),
        out_specs=(P("los", "tr"), P(), P(), P(), P()),
        check_vma=False,
    )
```

time: 1050 us -> 255 us (0.24); the launches traced: 1030 us -> 254 us
  local copies, waits for them, and re-layouts: 636 us -> 20 us
  other arithmetic: 172 us -> 5.39 us
  waiting for transfers between devices: 38.6 us -> 128 us
  Pallas kernels: 0 us -> 72.9 us
  matrix products: 68.4 us -> 0 us
  starting transfers between devices: 61.4 us -> 14.1 us
  blocking collectives: 37.5 us -> 0 us
    concatenate x24 -> x0, local copies, waits for them, and re-layouts: 277 us -> none  [the longest x12 209 us: plane_taps(): return jnp.concatenate(pieces, axis=-1)]
    gather x4 -> x0, local copies, waits for them, and re-layouts: 150 us -> none  [the longest x2 148 us: on_device(): rate_grad = jnp.take_along_axis(permuted_grad, targets, axis=2)]
    unnamed x7 -> x1, other arithmetic: 129 us -> 0.71 us
    unnamed x138 -> x6, local copies, waits for them, and re-layouts: 130 us -> 2.47 us
    psum x1, waiting for transfers between devices: 0.01 us -> 126 us  [on_device(): packed = lax.psum(packed, ('los', 'tr'))]
    pallas_call x0 -> x3, Pallas kernels: none -> 72.9 us  [the longest x1 30.6 us: on_device(): pl.pallas_call(functools.partial(backward_kernel, lines, rows_y), out_sha...]
    dot_general x13 -> x0, matrix products: 68.4 us -> none  [the longest x5 31.8 us: contract_rows(): lax.dot_general(left, right, (((0,), (0,)), ((), ())), preferred_element_...]
    ppermute x44 -> x6, starting transfers between devices: 61.4 us -> 14.1 us  [the longest x2 8.86 us: extended(): after = lax.ppermute(wide[:width], 'los', down)]
  transfers between devices with their start and end apart: 45 -> 7, of which waited for: 18 -> 3; matrix products, arithmetic and copies ran while one was open for 25% -> 5% of each run, Pallas kernels for 0% -> 0%
where the time goes in v1:
time: 255 us; the launch traced here: 254 us
  waiting for transfers between devices  128 us (50%)
  Pallas kernels  72.9 us (29%)
  local copies, waits for them, and re-layouts  20 us (8%)
  between operations  14.2 us (6%)
  starting transfers between devices  14.1 us (6%)
  other arithmetic  5.39 us (2%)
    psum x1, waiting for transfers between devices, on_device(): packed = lax.psum(packed, ('los', 'tr'))  126 us
    pallas_call x1, Pallas kernels, on_device(): pl.pallas_call(functools.partial(backward_kernel, lines, rows_y), out_sha...  30.6 us
    pallas_call x1, Pallas kernels, on_device(): pl.pallas_call(functools.partial(forward_kernel, lines, rows_y), out_shap...  21.4 us
    pallas_call x1, Pallas kernels, on_device(): pl.pallas_call(functools.partial(tile_kernel, total_cells), out_shape=[ja...  20.9 us
    ppermute x2, starting transfers between devices, extended(): after = lax.ppermute(wide[:width], 'los', down)  8.86 us
  transfers between devices with their start and end apart: 7, of which 3 were waited for; matrix products, arithmetic and copies ran while one was open for 5% of the time, Pallas kernels for 0%

profile of v1, /device:TPU:0, one launch (start us, length us, event | category | flops | bytes accessed | tf_op | source)
XLA Modules:
  0.0 254.4 jit_solution(9144674704220520595)
XLA Ops:
  7.2 0.0 copy-start
  7.2 0.0 all-reduce.5.cloned.1.call-start
  7.2 0.9 reshape.118
  8.2 3.0 %collective-permute-start = (bf16[16,3,48]{2,1,0:T(4,128)(2,1)S(1)}, bf16[16,3,48]{2,1,0:T(4,128)(2,1)S(1)}, u32[]{:S(2)}, u32[]{:S(2)}) collective-permute-start(bf16[16,3,48]{2,1,0:T(4,128)(2,1)S(1)} %slice_select_fusion), channel_id=1, source_target_pairs={{0,1},{1,0},{2,3},{3,2},{4,5},{5,4},{6,7},{7,6},{8,9},{9,8},{10,11... | collective-permute-start | bytes 13832 | tf_op jit(solution)/shard_map/ppermute | solution.py:325
  11.2 0.7 broadcast_multiply_fusion
  11.9 0.1 eq.40
  12.0 0.1 convert_reduce_fusion
  12.1 0.1 add.73
  12.2 0.1 select_reduce_fusion
  12.3 0.6 collective-permute-done
  12.9 0.1 fusion.9
  13.0 0.1 collective-permute-start.1
  13.1 4.4 %collective-permute-start.2 = (bf16[3,34,48]{2,1,0:T(8,128)(2,1)S(1)}, bf16[3,34,48]{2,1,0:T(8,128)(2,1)S(1)}, u32[]{:S(2)}, u32[]{:S(2)}) collective-permute-start(bf16[3,34,48]{2,1,0:T(8,128)(2,1)S(1)} %get-tuple-element.57), channel_id=1, source_target_pairs={{2,0},{4,2},{6,4},{8,6},{10,8},{12,10},{14,12},{16,14},{18,16},{20... | collective-permute-start | bytes 29384 | tf_op jit(solution)/shard_map/ppermute | solution.py:335
  17.5 0.7 reduce.2
  18.2 0.7 reshape.119.k3_ref
  18.9 1.6 copy.18.k2_ref
  20.6 0.1 convert_element_type.23
  20.6 0.1 mul.36
  20.7 1.5 reshape.121.target_ref
  22.3 1.5 reshape.122.count_ref
  23.8 0.6 pad.17.land_ref
  24.4 0.6 add.68.slot_ref
  24.9 0.0 collective-permute-done.1
  24.9 0.0 collective-permute-done.2
  24.9 0.9 maximum_convert_fusion.field_ref
  25.8 21.4 %forward.1 = (f32[16,24,48]{2,1,0:T(8,128)}, f32[16,32,1536]{2,1,0:T(8,128)}, f32[18,32,1536]{2,1,0:T(8,128)}, bf16[16,32,1536]{2,1,0:T(8,128)(2,1)}, bf16[16,32...) custom-call(f32[22,34,48]{2,1,0:T(8,128)} %maximum_convert_fusion.field_ref, bf16[27,32]{1,0:T(8,128)(2,1)} %k1_ref.1, ...), custom_call_target="tpu_custom_call" | custom-call | tf_op jit(solution)/shard_map/forward/pallas_call | solution.py:370
  47.2 1.7 reshape.120.rate_ref
  48.9 20.9 %tiles.1 = (f32[144,128]{1,0:T(8,128)}, f32[1,128]{1,0:T(1,128)}, bf16[144,128]{1,0:T(8,128)(2,1)}) custom-call(f32[144,128]{1,0:T(8,128)} %reshape.120.rate_ref, s32[144,128]{1,0:T(8,128)} %reshape.121.target_ref, s32[144,128]{1,0:T(8,128)} %reshape.122.count_ref, s32[1,144]{1,0:T(1,128)} %add.68.slot_ref, f32[13,128]{1,0:T(8,128)} %pad.17.land_ref), custom_call_target="tpu_custom_call" | custom-call | tf_op jit(solution)/shard_map/tiles/pallas_call | solution.py:397
  69.8 0.9 reshape.124
  70.8 2.1 collective-permute-start.3
  72.9 1.6 collective-permute-done.3
  74.5 0.1 fusion.11
  74.6 0.1 collective-permute-start.4
  74.7 4.4 %collective-permute-start.5 = (bf16[2,34,48]{2,1,0:T(8,128)(2,1)S(1)}, bf16[2,34,48]{2,1,0:T(8,128)(2,1)S(1)}, u32[]{:S(2)}, u32[]{:S(2)}) collective-permute-start(bf16[2,34,48]{2,1,0:T(8,128)(2,1)S(1)} %get-tuple-element.55), channel_id=1, source_target_pairs={{2,0},{4,2},{6,4},{8,6},{10,8},{12,10},{14,12},{16,14},{18,16},{20... | collective-permute-start | bytes 19592 | tf_op jit(solution)/shard_map/ppermute | solution.py:335
  79.1 1.3 rev.10.k3_ref
  80.4 0.0 copy-done
  80.4 0.2 reshape.125
  80.7 0.2 rev.9
  80.9 0.8 copy.19
  81.6 1.2 reduce_sum.32
  82.9 0.0 collective-permute-done.4
  82.9 0.0 collective-permute-done.5
  82.9 0.8 maximum_convert_fusion.1.grad_ref
  83.7 0.0 copy-start.1
  83.7 30.6 %backward.1 = f32[928,32]{1,0:T(8,128)} custom-call(f32[20,34,48]{2,1,0:T(8,128)} %maximum_convert_fusion.1.grad_ref, f32[16,32,1536]{2,1,0:T(8,128)} %get-tuple-element.29.pre1_ref, f32[18,32,1536]{2,1,0:T(8,128)} %get-tuple-element.30.pre2_ref, bf16[16,32,1536]{2,1,0:T(8,128)(2,1)} %get-tuple-element.31.h1_ref, ...), custom_call_target="tpu_custom_call" | custom-call | tf_op jit(solution)/shard_map/backward/pallas_call | solution.py:420
  114.2 1.9 scatter.4
  116.2 0.0 all-reduce.5.cloned.1.call-update
  116.2 0.0 copy-done.1
  116.2 0.6 reshape.123
  116.8 125.6 %all-reduce.5.cloned.1.call-done = f32[928,32]{1,0:T(8,128)} async-done(((f32[928,32]{1,0:T(8,128)}), f32[928,32]{1,0:T(8,128)}) %all-reduce.5.cloned.1.call-update) | async-done | bytes 118800 | tf_op jit(solution)/shard_map/psum | solution.py:439
  242.5 1.0 slice.77
  243.5 0.8 copy.20
  244.3 1.3 fusion.15
  245.7 0.7 reshape.128
  246.3 1.2 slice.75
  (9 shorter events, 0.1 us)
Async XLA Ops:
  7.2 73.3 %copy-start = (bf16[864,32]{0,1:T(8,128)(2,1)S(1)}, bf16[864,32]{0,1:T(8,128)(2,1)}, u32[]{:S(2)}) copy-start(bf16[864,32]{0,1:T(8,128)(2,1)} %param.14) | copy-start | bytes 165892
  7.2 235.3 %all-reduce.5.cloned.1.call-start = ((), (), s32[]{:S(2)}) async-start(), calls=%async_computation | async-start | bytes 950272 | tf_op jit(solution)/shard_map/psum | solution.py:439
  8.2 4.7 %collective-permute-start = (bf16[16,3,48]{2,1,0:T(4,128)(2,1)S(1)}, bf16[16,3,48]{2,1,0:T(4,128)(2,1)S(1)}, u32[]{:S(2)}, u32[]{:S(2)}) collective-permute-start(bf16[16,3,48]{2,1,0:T(4,128)(2,1)S(1)} %slice_select_fusion), channel_id=1, source_target_pairs={{0,1},{1,0},{2,3},{3,2},{4,5},{5,4},{6,7},{7,6},{8,9},{9,8},{10,11... | collective-permute-start | bytes 13832 | tf_op jit(solution)/shard_map/ppermute | solution.py:325
  13.0 11.9 %collective-permute-start.1 = (bf16[3,34,48]{2,1,0:T(8,128)(2,1)S(1)}, bf16[3,34,48]{2,1,0:T(8,128)(2,1)S(1)}, u32[]{:S(2)}, u32[]{:S(2)}) collective-permute-start(bf16[3,34,48]{2,1,0:T(8,128)(2,1)S(1)} %get-tuple-element.56), channel_id=1, source_target_pairs={{0,2},{2,4},{4,6},{6,8},{8,10},{10,12},{12,14},{14,16},{16,18},{18... | collective-permute-start | bytes 29384 | tf_op jit(solution)/shard_map/ppermute | solution.py:334
  13.1 11.8 %collective-permute-start.2 = (bf16[3,34,48]{2,1,0:T(8,128)(2,1)S(1)}, bf16[3,34,48]{2,1,0:T(8,128)(2,1)S(1)}, u32[]{:S(2)}, u32[]{:S(2)}) collective-permute-start(bf16[3,34,48]{2,1,0:T(8,128)(2,1)S(1)} %get-tuple-element.57), channel_id=1, source_target_pairs={{2,0},{4,2},{6,4},{8,6},{10,8},{12,10},{14,12},{16,14},{18,16},{20... | collective-permute-start | bytes 29384 | tf_op jit(solution)/shard_map/ppermute | solution.py:335
  70.8 3.7 %collective-permute-start.3 = (bf16[16,2,48]{2,1,0:T(2,128)(2,1)S(1)}, bf16[16,2,48]{2,1,0:T(2,128)(2,1)S(1)}, u32[]{:S(2)}, u32[]{:S(2)}) collective-permute-start(bf16[16,2,48]{2,1,0:T(2,128)(2,1)S(1)} %broadcast_select_fusion.1), channel_id=1, source_target_pairs={{0,1},{1,0},{2,3},{3,2},{4,5},{5,4},{6,7},{7,6},{8,9},{9,8},{10,11... | collective-permute-start | bytes 9224 | tf_op jit(solution)/shard_map/ppermute | solution.py:325
  74.6 8.2 %collective-permute-start.4 = (bf16[2,34,48]{2,1,0:T(8,128)(2,1)S(1)}, bf16[2,34,48]{2,1,0:T(8,128)(2,1)S(1)}, u32[]{:S(2)}, u32[]{:S(2)}) collective-permute-start(bf16[2,34,48]{2,1,0:T(8,128)(2,1)S(1)} %get-tuple-element.54), channel_id=1, source_target_pairs={{0,2},{2,4},{4,6},{6,8},{8,10},{10,12},{12,14},{14,16},{16,18},{18... | collective-permute-start | bytes 19592 | tf_op jit(solution)/shard_map/ppermute | solution.py:334
  74.7 8.2 %collective-permute-start.5 = (bf16[2,34,48]{2,1,0:T(8,128)(2,1)S(1)}, bf16[2,34,48]{2,1,0:T(8,128)(2,1)S(1)}, u32[]{:S(2)}, u32[]{:S(2)}) collective-permute-start(bf16[2,34,48]{2,1,0:T(8,128)(2,1)S(1)} %get-tuple-element.55), channel_id=1, source_target_pairs={{2,0},{4,2},{6,4},{8,6},{10,8},{12,10},{14,12},{16,14},{18,16},{20... | collective-permute-start | bytes 19592 | tf_op jit(solution)/shard_map/ppermute | solution.py:335
  83.7 32.5 %copy-start.1 = (f32[144,128]{1,0:T(8,128)S(1)}, f32[144,128]{1,0:T(8,128)}, u32[]{:S(2)}) copy-start(f32[144,128]{1,0:T(8,128)} %get-tuple-element.27) | copy-start | bytes 221188
Sparse Core Ops, SparseCore 0:
  116.3 126.0 all-reduce.4

commit v2 on v1

--- a/solution.py
+++ b/solution.py
@@ -11,9 +11,13 @@
 REACH = 6
 SPREAD = 2 * REACH + 1
 CAP = 24
+EDGE = 24
+SHARDS = 16
+SHARD = 16
 PITCH = 32
 SLOTS = SPREAD * PITCH
 HID = 32
+PACK = 29 * HID // 4
 YP = 32
 OFF = 4
 LANES = NZ * HID
@@ -31,6 +35,21 @@
 TN = (((0,), (0,)), ((), ()))
 
 
+def row_pieces():
+    pieces = []
+    for j in range(8):
+        done = 0
+        while done < NZ:
+            tile, first = divmod(j * NZ + done, 128)
+            length = min(NZ - done, 128 - first)
+            pieces.append((j, tile, first, done, length))
+            done += length
+    return pieces
+
+
+PIECES = row_pieces()
+
+
 def iota(shape, dim):
     return lax.broadcasted_iota(jnp.int32, shape, dim)
 
@@ -113,10 +132,20 @@
     return total
 
 
+def join_rows(out_ref, own, after, before):
+    rows = own.shape[1]
+    position = lax.axis_index("tr")
+    low = before[:, 8 - OFF - 1 :]
+    high = after[:, : YP + 2 - OFF - 1 - rows]
+    out_ref[:, 0 : OFF + 1, :] = jnp.where(position == 1, low, 0.0)
+    out_ref[:, OFF + 1 : OFF + 1 + rows, :] = own
+    out_ref[:, OFF + 1 + rows : YP + 2, :] = jnp.where(position == 0, high, 0.0)
+
+
 def forward_kernel(
     lines, rows_y, field_ref, k1_ref, k2_ref, k3_ref,
     rate_ref, pre1_ref, pre2_ref, h1_ref, h2_ref, taps_ref,
-    d9, w1, w2, w3, h1b, h2, z9,
+    d9, w1, w2, w3, h1b, h2, z9, cells,
 ):
     l2, l1 = lines + 4, lines + 2
     fill_thin_band(k1_ref[...], w1, False)
@@ -158,13 +187,22 @@
         a, b = ab // 3, ab % 3
         row = OFF - 1 + b
         total = total + z9[a : a + lines, row : row + rows_y, ab * NZ : (ab + 1) * NZ]
-    rate_ref[...] = jnp.exp(total)
+    cells[...] = jnp.exp(total).reshape(lines * rows_y, NZ)
+    groups = lines * rows_y // 8
+    for tile in range(3):
+        parts = [
+            cells[pl.ds(j, groups, stride=8), :][:, start : start + length]
+            for j, at, _, start, length in PIECES
+            if at == tile
+        ]
+        rate_ref[pl.ds(tile, groups, stride=3), :] = jnp.concatenate(parts, axis=1)
 
 
 def tile_kernel(
     total_cells, rate_ref, target_ref, count_ref, slot_ref, land_ref,
-    red_ref, loss_ref, grad_ref,
-    msg, recv, back, ret, marks, send_sem, recv_sem, send_back, recv_back,
+    red_ref, loss_ref, main_ref, side_ref,
+    msg, recv, back, ret, marks, grad, main, side,
+    send_sem, recv_sem, send_back, recv_back, send_halo, recv_halo,
 ):
     tiles = rate_ref.shape[0]
     me, other = lax.axis_index("los"), lax.axis_index("tr")
@@ -177,6 +215,9 @@
     barrier = pltpu.get_barrier_semaphore()
     for d in distances:
         pl.semaphore_signal(barrier, inc=1, device_id=peer(d - REACH), device_id_type=MESH)
+    across = [(lax.rem(me + k + size, size), 1 - other) for k in (-1, 0, 1)]
+    for device in across:
+        pl.semaphore_signal(barrier, inc=1, device_id=device, device_id_type=MESH)
 
     def add_tile(t, perm):
         hit = iota((128, 128), 0) == target_ref[pl.ds(t, 1), :]
@@ -190,7 +231,7 @@
     landing = land_ref[...].reshape(SPREAD, 1, 128)
     msg[...] = jnp.where(iota((SPREAD, PITCH, 128), 1) == CAP, landing, sent)
 
-    pl.semaphore_wait(barrier, len(distances))
+    pl.semaphore_wait(barrier, len(distances) + 3)
     copies = []
     for d in distances:
         copy = pltpu.make_async_remote_copy(
@@ -235,12 +276,34 @@
         pick, ret[...].reshape(SLOTS, 128), TN, precision=HIGH, preferred_element_type=F32
     )
     picked = jnp.take_along_axis(moved, target_ref[...], axis=1)
-    grad_ref[...] = (picked * rate_ref[...]).astype(BF16)
-    for copy in copies + returns:
+    grad[...] = (picked * rate_ref[...]).astype(BF16).astype(F32)
+    halo = []
+    top = grad.at[tiles - EDGE : tiles]
+    bottom = grad.at[0:EDGE]
+    for n, (source, target, device) in enumerate([
+        (top, main.at[0], peer(1)),
+        (bottom, main.at[1], peer(-1)),
+        (top, side.at[0:EDGE], across[2]),
+        (bottom, side.at[EDGE + tiles : 2 * EDGE + tiles], across[0]),
+        (grad, side.at[EDGE : EDGE + tiles], across[1]),
+    ]):
+        copy = pltpu.make_async_remote_copy(
+            src_ref=source, dst_ref=target, send_sem=send_halo.at[n], recv_sem=recv_halo.at[n],
+            device_id=device, device_id_type=MESH,
+        )
+        copy.start()
+        halo.append(copy)
+    main_ref[EDGE : EDGE + tiles, :] = grad[...]
+    for copy in halo:
+        copy.wait_recv()
+    main_ref[0:EDGE, :] = main[0]
+    main_ref[EDGE + tiles : 2 * EDGE + tiles, :] = main[1]
+    side_ref[...] = side[...]
+    for copy in copies + returns + halo:
         copy.wait_send()
 
 
-def thin_extract(product, fold):
+def thin_extract(product, fold, turned):
     diff = iota((NZ, LANES), 0) - (iota((NZ, LANES), 1) >> 5)
     rows = []
     for ab in range(9):
@@ -249,6 +312,7 @@
             rows.append(
                 jnp.sum(jnp.where(diff == c - 1, block, 0.0), axis=0, keepdims=True)
             )
+    rows = rows[::-1] if turned else rows
     rows = jnp.concatenate(rows + [jnp.zeros((5, LANES), F32)], axis=0)
     return jnp.dot(rows, fold, precision=HIGH, preferred_element_type=F32)
 
@@ -258,14 +322,29 @@
 
 
 def backward_kernel(
-    lines, rows_y, grad_ref, pre1_ref, pre2_ref, h1_ref, h2_ref, taps_ref, k2_ref, k3_ref,
+    lines, rows_y, main_ref, side_ref, pre1_ref, pre2_ref, h1_ref, h2_ref, taps_ref, k2_ref, k3_ref,
     out_ref,
-    g9, w2, w3, a2b, a1, h1t, prod, sums,
+    g9, w2, w3, a2b, a1, h1t, prod, sums, cells, wide,
 ):
     l1 = lines + 2
     fill_wide_band(k2_ref[...], w2)
     fill_thin_band(k3_ref[...], w3, False)
-    fill_taps(grad_ref, g9, l1)
+    l2 = lines + 4
+    groups = l2 * rows_y // 8
+    skip = EDGE - 6 * rows_y // 8
+    for source, source_ref in enumerate((main_ref, side_ref)):
+        for j in range(8):
+            parts = [
+                source_ref[pl.ds(skip + tile, groups, stride=3), :][:, first : first + length]
+                for at, tile, first, _, length in PIECES
+                if at == j
+            ]
+            row = parts[0] if len(parts) == 1 else jnp.concatenate(parts, axis=1)
+            cells[source, pl.ds(j, groups, stride=8), :] = row
+    own = cells[0].reshape(l2, rows_y, NZ)
+    other = cells[1].reshape(l2, rows_y, NZ)
+    join_rows(wide, own, other[:, :8], other[:, rows_y - 8 :])
+    fill_taps(wide, g9, l1)
     clear_pads(a2b)
 
     @pl.loop(0, GROUPS)
@@ -290,12 +369,12 @@
     prod[...] = lax.dot_general(
         taps_ref[...], a1[...].reshape(lines * YP, LANES), TN, preferred_element_type=F32
     )
-    out_ref[27 * HID : 28 * HID, :] = thin_extract(prod, fold)
+    out_ref[27 * HID : 28 * HID, :] = thin_extract(prod, fold, False)
     prod[...] = lax.dot_general(
         g9[1 : 1 + lines].reshape(lines * YP, 9 * NZ).astype(BF16),
         h2_ref[...].reshape(lines * YP, LANES), TN, preferred_element_type=F32,
     )
-    out_ref[28 * HID : 29 * HID, :] = thin_extract(prod, fold)
+    out_ref[28 * HID : 29 * HID, :] = thin_extract(prod, fold, True)
 
     lane_z = iota((HID, 2 * GROUP), 1) >> 5
     for ab in range(9):
@@ -317,23 +396,116 @@
     )
 
 
-def extended(block, width):
-    lines, rows, depth = block.shape
-    position = lax.axis_index("tr")
+def halo_kernel(
+    lines, rows_y, width, own_ref, out_ref, stage, low, high, side, side_low, side_high,
+    send_sem, recv_sem,
+):
+    me, other = lax.axis_index("los"), lax.axis_index("tr")
     size = lax.axis_size("los")
-    send = jnp.where(position == 0, block[:, rows - width :], block[:, :width])
-    got = lax.ppermute(send, "tr", [(0, 1), (1, 0)])
-    none = jnp.zeros_like(got)
-    gap = OFF + 1 - width
-    low = jnp.where(position == 1, got, none)
-    high = jnp.where(position == 0, got, none)
-    wide = jnp.concatenate([low, block, high], axis=1)
-    wide = jnp.pad(wide, ((0, 0), (gap, YP + 2 - gap - rows - 2 * width), (0, 0)))
-    up = [(i, (i + 1) % size) for i in range(size)]
-    down = [(j, i) for i, j in up]
-    before = lax.ppermute(wide[lines - width :], "los", up)
-    after = lax.ppermute(wide[:width], "los", down)
-    return jnp.concatenate([before, wide, after], axis=0).astype(F32)
+    up, down = lax.rem(me + 1, size), lax.rem(me + size - 1, size)
+    barrier = pltpu.get_barrier_semaphore()
+    devices = [(up, other), (down, other), (me, 1 - other), (up, 1 - other), (down, 1 - other)]
+    for device in devices:
+        pl.semaphore_signal(barrier, inc=1, device_id=device, device_id_type=MESH)
+    own = own_ref[...].reshape(lines, rows_y, NZ)
+    stage[...] = jnp.where(other == 0, own[:, rows_y - 8 :], own[:, :8])
+    pl.semaphore_wait(barrier, len(devices))
+    parts = [
+        (own_ref.at[(lines - width) * rows_y : lines * rows_y], low),
+        (own_ref.at[0 : width * rows_y], high),
+        (stage, side),
+        (stage.at[lines - width : lines], side_low),
+        (stage.at[0:width], side_high),
+    ]
+    copies = []
+    for n, (source, target) in enumerate(parts):
+        copy = pltpu.make_async_remote_copy(
+            src_ref=source, dst_ref=target, send_sem=send_sem.at[n], recv_sem=recv_sem.at[n],
+            device_id=devices[n], device_id_type=MESH,
+        )
+        copy.start()
+        copies.append(copy)
+    for copy in copies:
+        copy.wait_recv()
+    near, far = low[...].reshape(width, rows_y, NZ), high[...].reshape(width, rows_y, NZ)
+    join_rows(out_ref.at[0:width], near, side_low[...], side_low[...])
+    join_rows(out_ref.at[width : width + lines], own, side[...], side[...])
+    join_rows(out_ref.at[width + lines : 2 * width + lines], far, side_high[...], side_high[...])
+    for copy in copies:
+        copy.wait_send()
+
+
+def sum_kernel(
+    in_ref, loss_ref, out_ref, total_ref, mine, parts, pairs, done,
+    send_one, recv_one, send_two, recv_two, send_three, recv_three,
+):
+    me, other = lax.axis_index("los"), lax.axis_index("tr")
+    blocks = lax.axis_size("los") // SHARDS
+    block, shard = me // SHARDS, lax.rem(me, SHARDS)
+    barrier = pltpu.get_barrier_semaphore()
+    group = [
+        (block * SHARDS + lax.rem(shard + k, SHARDS), other) for k in range(1, SHARDS)
+    ]
+    count = 2 * blocks
+    index = block * 2 + other
+    column = []
+    for k in range(1, count):
+        peer = lax.rem(index + k, count)
+        column.append(((peer // 2) * SHARDS + shard, lax.rem(peer, 2)))
+    for device in group + column:
+        pl.semaphore_signal(barrier, inc=1, device_id=device, device_id_type=MESH)
+    for q in range(4):
+        mine[0:PACK, q * HID : (q + 1) * HID] = in_ref[q * PACK : (q + 1) * PACK, :]
+    rest = SHARDS * SHARD - PACK
+    mine[PACK : SHARDS * SHARD, :] = jnp.where(iota((rest, 128), 0) == 0, loss_ref[...], 0.0)
+    pl.semaphore_wait(barrier, len(group) + len(column))
+
+    def rows(k):
+        start = lax.rem(shard + k, SHARDS) * SHARD
+        return pl.ds(pl.multiple_of(start, SHARD), SHARD)
+
+    copies = []
+
+    def send(source, target, sends, recvs, n, device):
+        copy = pltpu.make_async_remote_copy(
+            src_ref=source, dst_ref=target, send_sem=sends.at[n], recv_sem=recvs.at[n],
+            device_id=device, device_id_type=MESH,
+        )
+        copy.start()
+        copies.append(copy)
+        return copy
+
+    first = [
+        send(mine.at[rows(k)], parts.at[k], send_one, recv_one, k, group[k - 1])
+        for k in range(1, SHARDS)
+    ]
+    total = mine[rows(0), :]
+    for k in range(1, SHARDS):
+        first[k - 1].wait_recv()
+        total = total + parts[k]
+    parts[0] = total
+    second = [
+        send(parts.at[0], pairs.at[index], send_two, recv_two, k, column[k - 1])
+        for k in range(1, count)
+    ]
+    pairs[index] = total
+    for copy in second:
+        copy.wait_recv()
+    total = pairs[0]
+    for k in range(1, count):
+        total = total + pairs[k]
+    done[rows(0), :] = total
+    third = [
+        send(done.at[rows(0)], done.at[rows(0)], send_three, recv_three, k, group[k - 1])
+        for k in range(1, SHARDS)
+    ]
+    for copy in third:
+        copy.wait_recv()
+    for q in range(4):
+        out_ref[q * PACK : (q + 1) * PACK, :] = done[0:PACK, q * HID : (q + 1) * HID]
+    total_ref[...] = jnp.sum(done[PACK : PACK + 1, :], axis=1, keepdims=True)
+    for copy in copies:
+        copy.wait_send()
 
 
 def on_device(
@@ -366,11 +538,27 @@
         marks.astype(F32).reshape(SPREAD, PITCH), ((0, 0), (0, 128 - PITCH)), constant_values=-1.0
     )
 
-    field = extended(density.reshape(lines, rows_y, NZ), 3)
+    five = pltpu.SemaphoreType.DMA((5,))
+    corner = pltpu.VMEM((3, 8, NZ), F32)
+    field = pl.pallas_call(
+        functools.partial(halo_kernel, lines, rows_y, 3),
+        out_shape=jax.ShapeDtypeStruct((lines + 6, YP + 2, NZ), F32),
+        in_specs=[vmem],
+        out_specs=vmem,
+        scratch_shapes=[
+            pltpu.VMEM((lines, 8, NZ), F32),
+            pltpu.VMEM((3 * rows_y, NZ), F32),
+            pltpu.VMEM((3 * rows_y, NZ), F32),
+            pltpu.VMEM((lines, 8, NZ), F32),
+            corner, corner, five, five,
+        ],
+        compiler_params=pltpu.CompilerParams(collective_id=1, has_side_effects=True),
+        name="halo",
+    )(density.astype(F32).reshape(lines * rows_y, NZ))
     rate, pre1, pre2, h1, h2, taps = pl.pallas_call(
         functools.partial(forward_kernel, lines, rows_y),
         out_shape=[
-            jax.ShapeDtypeStruct((lines, rows_y, NZ), F32),
+            jax.ShapeDtypeStruct((tiles, 128), F32),
             jax.ShapeDtypeStruct((lines, YP, LANES), F32),
             jax.ShapeDtypeStruct((l1, YP, LANES), F32),
             jax.ShapeDtypeStruct((lines, YP, LANES), BF16),
@@ -387,6 +575,7 @@
             pltpu.VMEM((3, l2, YP, WIDE), BF16),
             pltpu.VMEM((l1, YP, LANES), BF16),
             pltpu.VMEM((l1, YP, 9 * NZ), F32),
+            pltpu.VMEM((lines * rows_y, NZ), F32),
         ],
         compiler_params=pltpu.CompilerParams(vmem_limit_bytes=LIMIT),
         name="forward",
@@ -394,33 +583,40 @@
 
     box = pltpu.VMEM((SPREAD, PITCH, 128), F32)
     sems = pltpu.SemaphoreType.DMA((SPREAD,))
-    redshift_rate, loss_part, log_grad = pl.pallas_call(
+    redshift_rate, loss_part, grad_main, grad_side = pl.pallas_call(
         functools.partial(tile_kernel, total_cells),
         out_shape=[
             jax.ShapeDtypeStruct((tiles, 128), F32),
             jax.ShapeDtypeStruct((1, 128), F32),
-            jax.ShapeDtypeStruct((tiles, 128), BF16),
+            jax.ShapeDtypeStruct((tiles + 2 * EDGE, 128), F32),
+            jax.ShapeDtypeStruct((tiles + 2 * EDGE, 128), F32),
         ],
         in_specs=[vmem] * 5,
-        out_specs=[vmem] * 3,
-        scratch_shapes=[box, box, box, box, pltpu.VMEM((8, 512), F32), sems, sems, sems, sems],
+        out_specs=[vmem] * 4,
+        scratch_shapes=[
+            box, box, box, box,
+            pltpu.VMEM((8, 512), F32),
+            pltpu.VMEM((tiles, 128), F32),
+            pltpu.VMEM((2, EDGE, 128), F32),
+            pltpu.VMEM((tiles + 2 * EDGE, 128), F32),
+            sems, sems, sems, sems, five, five,
+        ],
         compiler_params=pltpu.CompilerParams(
             vmem_limit_bytes=LIMIT, collective_id=0, has_side_effects=True
         ),
         name="tiles",
     )(
-        rate.reshape(tiles, 128),
+        rate,
         cell_targets.reshape(tiles, 128),
         observed_counts.reshape(tiles, 128),
         slot.reshape(1, tiles),
         marks,
     )
 
-    grad = extended(log_grad.reshape(lines, rows_y, NZ), 2)
     packed = pl.pallas_call(
         functools.partial(backward_kernel, lines, rows_y),
         out_shape=jax.ShapeDtypeStruct((29 * HID, HID), F32),
-        in_specs=[vmem] * 8,
+        in_specs=[vmem] * 9,
         out_specs=vmem,
         scratch_shapes=[
             pltpu.VMEM((l1, YP, 9 * NZ), F32),
@@ -431,18 +627,39 @@
             pltpu.VMEM((GROUPS, GROUP, lines * YP), BF16),
             pltpu.VMEM((9 * NZ, LANES), F32),
             pltpu.VMEM((27 * HID, 2 * GROUP), F32),
+            pltpu.VMEM((2, l2 * rows_y, NZ), F32),
+            pltpu.VMEM((l2, YP + 2, NZ), F32),
         ],
         compiler_params=pltpu.CompilerParams(vmem_limit_bytes=LIMIT),
         name="backward",
-    )(grad, pre1, pre2, h1, h2, taps, second_back, third[::-1])
-    packed = packed.at[29 * HID - 1, 0].set(jnp.sum(loss_part))
-    packed = lax.psum(packed, ("los", "tr"))
+    )(grad_main, grad_side, pre1, pre2, h1, h2, taps, second_back, third[::-1])
+    blocks = lax.axis_size("los") // SHARDS
+    piece = pltpu.SemaphoreType.DMA((SHARDS,))
+    pair = pltpu.SemaphoreType.DMA((2 * blocks,))
+    packed, loss = pl.pallas_call(
+        sum_kernel,
+        out_shape=[
+            jax.ShapeDtypeStruct((29 * HID, HID), F32),
+            jax.ShapeDtypeStruct((1, 1), F32),
+        ],
+        in_specs=[vmem] * 2,
+        out_specs=[vmem] * 2,
+        scratch_shapes=[
+            pltpu.VMEM((SHARDS * SHARD, 128), F32),
+            pltpu.VMEM((SHARDS, SHARD, 128), F32),
+            pltpu.VMEM((2 * blocks, SHARD, 128), F32),
+            pltpu.VMEM((SHARDS * SHARD, 128), F32),
+            piece, piece, pair, pair, piece, piece,
+        ],
+        compiler_params=pltpu.CompilerParams(collective_id=2, has_side_effects=True),
+        name="sum",
+    )(packed, loss_part)
     return (
         redshift_rate.reshape(lines, plane),
-        packed[29 * HID - 1, 0],
+        loss.reshape(()),
         packed[27 * HID : 27 * HID + 27],
         packed[: 27 * HID],
-        packed[28 * HID : 28 * HID + 27][::-1].reshape(27 * HID, 1),
+        packed[28 * HID : 28 * HID + 27].reshape(27 * HID, 1),
     )
 
 

time: 255 us -> 129 us (0.51)
  waiting for transfers between devices: 128 us -> 0 us
  Pallas kernels: 72.9 us -> 107 us
  starting transfers between devices: 14.1 us -> 0 us
  between operations: 14.2 us -> 2.47 us
  local copies, waits for them, and re-layouts: 20 us -> 15.7 us
  other arithmetic: 5.39 us -> 2.24 us
    psum x1 -> x0, waiting for transfers between devices: 126 us -> none  [on_device(): packed = lax.psum(packed, ('los', 'tr'))]
    pallas_call x0 -> x2, Pallas kernels: none -> 27.6 us  [the longest x1 16.6 us: on_device(): pl.pallas_call(sum_kernel, out_shape=[jax.ShapeDtypeStruct((29 * HID, HID...]
    ppermute x6 -> x0, starting transfers between devices: 14.1 us -> none  [the longest x2 8.86 us: extended(): after = lax.ppermute(wide[:width], 'los', down)]
    pallas_call x1, Pallas kernels: 20.9 us -> 27.6 us  [on_device(): pl.pallas_call(functools.partial(tile_kernel, total_cells), out_shape=[ja...]
  transfers between devices with their start and end apart: 7 -> 0, of which waited for: 3 -> 0; matrix products, arithmetic and copies ran while one was open for 5% -> 0% of each run, Pallas kernels for 0% -> 0%
where the time goes in v2:
time: 129 us; the launch traced here: 128 us
  Pallas kernels  107 us (83%)
  local copies, waits for them, and re-layouts  15.7 us (12%)
  between operations  2.47 us (2%)
  other arithmetic  2.24 us (2%)
    pallas_call x1, Pallas kernels, on_device(): pl.pallas_call(functools.partial(backward_kernel, lines, rows_y), out_sha...  30.9 us
    pallas_call x1, Pallas kernels, on_device(): pl.pallas_call(functools.partial(tile_kernel, total_cells), out_shape=[ja...  27.6 us
    pallas_call x1, Pallas kernels, on_device(): pl.pallas_call(functools.partial(forward_kernel, lines, rows_y), out_shap...  21.3 us
    pallas_call x1, Pallas kernels, on_device(): pl.pallas_call(sum_kernel, out_shape=[jax.ShapeDtypeStruct((29 * HID, HID...  16.6 us
    pallas_call x1, Pallas kernels, on_device(): pl.pallas_call(functools.partial(halo_kernel, lines, rows_y, 3), out_shap...  11 us

profile of v2, /device:TPU:0, one launch (start us, length us, event | category | flops | bytes accessed | tf_op | source)
XLA Modules:
  0.0 127.9 jit_solution(14253434446739243983)
XLA Ops:
  0.6 0.7 broadcast_multiply_fusion
  1.3 0.1 eq.28
  1.4 0.1 convert_reduce_fusion
  1.6 0.1 add.65
  1.6 0.1 select_reduce_fusion
  1.8 0.1 convert_element_type.13
  1.9 0.6 pad.4.land_ref
  2.5 0.7 reduce
  3.2 0.7 reshape.86.k3_ref
  3.9 1.6 %reshape.95.own_ref = f32[384,48]{1,0:T(8,128)} reshape(bf16[16,1152]{1,0:T(8,128)(2,1)} %param.7) | data formatting | bytes 110592 | tf_op jit(solution)/shard_map/reshape | solution.py:557
  5.4 11.0 %halo.1.field_ref = f32[22,34,48]{2,1,0:T(8,128)} custom-call(f32[384,48]{1,0:T(8,128)} %reshape.95.own_ref), custom_call_target="tpu_custom_call" | custom-call | tf_op jit(solution)/shard_map/halo/pallas_call | solution.py:543
  16.5 1.7 %copy.18.k2_ref = bf16[864,32]{1,0:T(8,128)(2,1)} copy(bf16[864,32]{0,1:T(8,128)(2,1)} %param.12) | data formatting | bytes 110592 | tf_op args[5]
  18.1 21.3 %forward.1 = (f32[144,128]{1,0:T(8,128)}, f32[16,32,1536]{2,1,0:T(8,128)}, f32[18,32,1536]{2,1,0:T(8,128)}, bf16[16,32,1536]{2,1,0:T(8,128)(2,1)}, bf16[16,32,15...) custom-call(f32[22,34,48]{2,1,0:T(8,128)} %halo.1.field_ref, bf16[27,32]{1,0:T(8,128)(2,1)} %k1_ref.1, ...), custom_call_target="tpu_custom_call" | custom-call | tf_op jit(solution)/shard_map/forward/pallas_call | solution.py:558
  39.5 0.1 mul.36
  39.6 0.6 add.60.slot_ref
  40.1 1.5 %reshape.87.target_ref = s32[144,128]{1,0:T(8,128)} reshape(s32[16,1152]{1,0:T(8,128)} %param.9) | data formatting | bytes 147456 | tf_op jit(solution)/shard_map/reshape | solution.py:610
  41.6 1.5 %reshape.88.count_ref = s32[144,128]{1,0:T(8,128)} reshape(s32[16,1152]{1,0:T(8,128)} %param.8) | data formatting | bytes 147456 | tf_op jit(solution)/shard_map/reshape | solution.py:611
  43.2 27.6 %tiles.1 = (f32[144,128]{1,0:T(8,128)}, f32[1,128]{1,0:T(1,128)}, f32[192,128]{1,0:T(8,128)}, f32[192,128]{1,0:T(8,128)}) custom-call(f32[144,128]{1,0:T(8,128)} %get-tuple-element.17.rate_ref, s32[144,128]{1,0:T(8,128)} %reshape.87.target_ref, s32[144,128]{1,0:T(8,128)} %reshape.88.count_ref, s32[1,144]{1,0:T(1,128)} %add.60.slot_ref, f32[13,128]{1,0:T(8,128)} %pad.4.land_ref), custom_call_target="tpu_custom_call" | custom-call | tf_op jit(solution)/shard_map/tiles/pallas_call | solution.py:586
  70.8 1.3 %rev.7.k3_ref = bf16[27,32]{1,0:T(8,128)(2,1)} reverse(bf16[27,32]{1,0:T(8,128)(2,1)} %reshape.86.k3_ref), dimensions={0} | reverse | bytes 3456 | tf_op jit(solution)/shard_map/rev | solution.py:635
  72.1 1.0 reshape.90
  73.1 0.2 rev.6
  73.3 0.8 copy.19
  74.1 0.0 copy-start
  74.1 30.9 %backward.1.in_ref = f32[928,32]{1,0:T(8,128)} custom-call(f32[192,128]{1,0:T(8,128)} %get-tuple-element.19.main_ref, f32[192,128]{1,0:T(8,128)} %get-tuple-element.20.side_ref, f32[16,32,1536]{2,1,0:T(8,128)} %get-tuple-element.21.pre1_ref, f32[18,32,1536]{2,1,0:T(8,128)} %get-tuple-element.22.pre2_ref, bf16[16,32,1536]{2,1,0:T(8,128)(2,1)} %get-tuple-element.23.h1_ref, ...), custom_call_target="tpu_custom_call" | custom-call | tf_op jit(solution)/shard_map/backward/pallas_call | solution.py:616
  105.0 16.6 %sum.1 = (f32[928,32]{1,0:T(8,128)}, f32[1,1]{1,0:T(1,128)}) custom-call(f32[928,32]{1,0:T(8,128)} %backward.1.in_ref, f32[1,128]{1,0:T(1,128)} %get-tuple-element.26.loss_ref), custom_call_target="tpu_custom_call" | custom-call | tf_op jit(solution)/shard_map/sum/pallas_call | solution.py:639
  121.6 1.0 slice.10
  122.7 0.8 copy.20
  123.5 1.3 %fusion.3 = (f32[27,32]{1,0:T(8,128)S(1)}, f32[27,32]{1,0:T(8,128)}) fusion(f32[928,32]{1,0:T(8,128)} %get-tuple-element.28), kind=kLoop, calls=%fused_computation.18 | loop fusion | bytes 13824 | tf_op jit(solution)/shard_map/slice | solution.py:662
  124.8 0.7 reshape.93
  125.5 0.0 copy-done
  125.5 0.6 reshape.89
  (2 shorter events, 0.0 us)
Async XLA Ops:
  74.1 51.4 %copy-start = (f32[144,128]{1,0:T(8,128)S(1)}, f32[144,128]{1,0:T(8,128)}, u32[]{:S(2)}) copy-start(f32[144,128]{1,0:T(8,128)} %get-tuple-element.18) | copy-start | bytes 221188

commit v3 on v2

--- a/solution.py
+++ b/solution.py
@@ -59,7 +59,7 @@
     return jnp.dot(kernel, rep.astype(BF16), preferred_element_type=F32)
 
 
-def fill_thin_band(kernel, out_ref, flip):
+def fill_thin_band(kernel, out_ref, flip, turned=False):
     tiled = repeat_lanes(kernel, LANES)
     diff = iota((NZ, LANES), 0) - (iota((NZ, LANES), 1) >> 5)
     if flip:
@@ -67,7 +67,7 @@
     for ab in range(9):
         block = jnp.zeros((NZ, LANES), F32)
         for c in range(3):
-            row = 3 * ab + c
+            row = 26 - 3 * ab - c if turned else 3 * ab + c
             block = jnp.where(diff == c - 1, tiled[row : row + 1, :], block)
         out_ref[ab * NZ : (ab + 1) * NZ, :] = block.astype(BF16)
 
@@ -328,7 +328,7 @@
 ):
     l1 = lines + 2
     fill_wide_band(k2_ref[...], w2)
-    fill_thin_band(k3_ref[...], w3, False)
+    fill_thin_band(k3_ref[...], w3, False, True)
     l2 = lines + 4
     groups = l2 * rows_y // 8
     skip = EDGE - 6 * rows_y // 8
@@ -436,7 +436,7 @@
 
 
 def sum_kernel(
-    in_ref, loss_ref, out_ref, total_ref, mine, parts, pairs, done,
+    in_ref, loss_ref, first_ref, second_ref, third_ref, total_ref, out_ref, mine, parts, pairs, done,
     send_one, recv_one, send_two, recv_two, send_three, recv_three,
 ):
     me, other = lax.axis_index("los"), lax.axis_index("tr")
@@ -503,6 +503,9 @@
         copy.wait_recv()
     for q in range(4):
         out_ref[q * PACK : (q + 1) * PACK, :] = done[0:PACK, q * HID : (q + 1) * HID]
+    second_ref[...] = out_ref[0 : 27 * HID, :]
+    first_ref[...] = out_ref[27 * HID : 27 * HID + 27, :]
+    third_ref[...] = out_ref[28 * HID : 28 * HID + 27, :]
     total_ref[...] = jnp.sum(done[PACK : PACK + 1, :], axis=1, keepdims=True)
     for copy in copies:
         copy.wait_send()
@@ -632,19 +635,22 @@
         ],
         compiler_params=pltpu.CompilerParams(vmem_limit_bytes=LIMIT),
         name="backward",
-    )(grad_main, grad_side, pre1, pre2, h1, h2, taps, second_back, third[::-1])
+    )(grad_main, grad_side, pre1, pre2, h1, h2, taps, second_back, third)
     blocks = lax.axis_size("los") // SHARDS
     piece = pltpu.SemaphoreType.DMA((SHARDS,))
     pair = pltpu.SemaphoreType.DMA((2 * blocks,))
-    packed, loss = pl.pallas_call(
+    grad_first, grad_second, grad_third, loss = pl.pallas_call(
         sum_kernel,
         out_shape=[
-            jax.ShapeDtypeStruct((29 * HID, HID), F32),
+            jax.ShapeDtypeStruct((27, HID), F32),
+            jax.ShapeDtypeStruct((27 * HID, HID), F32),
+            jax.ShapeDtypeStruct((27, HID), F32),
             jax.ShapeDtypeStruct((1, 1), F32),
         ],
         in_specs=[vmem] * 2,
-        out_specs=[vmem] * 2,
+        out_specs=[vmem] * 4,
         scratch_shapes=[
+            pltpu.VMEM((29 * HID, HID), F32),
             pltpu.VMEM((SHARDS * SHARD, 128), F32),
             pltpu.VMEM((SHARDS, SHARD, 128), F32),
             pltpu.VMEM((2 * blocks, SHARD, 128), F32),
@@ -657,9 +663,9 @@
     return (
         redshift_rate.reshape(lines, plane),
         loss.reshape(()),
-        packed[27 * HID : 27 * HID + 27],
-        packed[: 27 * HID],
-        packed[28 * HID : 28 * HID + 27].reshape(27 * HID, 1),
+        grad_first,
+        grad_second,
+        grad_third.reshape(27 * HID, 1),
     )
 
 

time: 129 us -> 128 us (level)
    slice x2 -> x0, local copies, waits for them, and re-layouts: 2.38 us -> none  [the longest x1 1.34 us: on_device(): packed[28 * HID:28 * HID + 27].reshape(27 * HID, 1)]
    unnamed x4 -> x5, local copies, waits for them, and re-layouts: 2.48 us -> 4.82 us
    rev x1 -> x0, local copies, waits for them, and re-layouts: 1.31 us -> none  [on_device(): third[::-1]]
where the time goes in v3:
time: 128 us; the launch traced here: 127 us
  Pallas kernels  107 us (84%)
  local copies, waits for them, and re-layouts  15.1 us (12%)
  between operations  2.46 us (2%)
  other arithmetic  2.24 us (2%)
    pallas_call x1, Pallas kernels, on_device(): pl.pallas_call(functools.partial(backward_kernel, lines, rows_y), out_sha...  30.9 us
    pallas_call x1, Pallas kernels, on_device(): pl.pallas_call(functools.partial(tile_kernel, total_cells), out_shape=[ja...  27.6 us
    pallas_call x1, Pallas kernels, on_device(): pl.pallas_call(functools.partial(forward_kernel, lines, rows_y), out_shap...  21.3 us
    pallas_call x1, Pallas kernels, on_device(): pl.pallas_call(sum_kernel, out_shape=[jax.ShapeDtypeStruct((27, HID), F32...  16.6 us
    pallas_call x1, Pallas kernels, on_device(): pl.pallas_call(functools.partial(halo_kernel, lines, rows_y, 3), out_shap...  11 us
    unnamed x5, local copies, waits for them, and re-layouts  4.82 us

profile of v3, /device:TPU:0, one launch (start us, length us, event | category | flops | bytes accessed | tf_op | source)
XLA Modules:
  0.0 127.3 jit_solution(7873192178157199037)
XLA Ops:
  0.6 0.7 broadcast_multiply_fusion
  1.3 0.1 eq.28
  1.4 0.1 convert_reduce_fusion
  1.6 0.1 add.65
  1.6 0.1 select_reduce_fusion
  1.8 0.1 convert_element_type.13
  1.9 0.6 pad.4.land_ref
  2.5 0.7 reduce
  3.2 0.7 reshape.86.k3_ref
  3.9 1.6 %reshape.95.own_ref = f32[384,48]{1,0:T(8,128)} reshape(bf16[16,1152]{1,0:T(8,128)(2,1)} %param.7) | data formatting | bytes 110592 | tf_op jit(solution)/shard_map/reshape | solution.py:560
  5.4 11.0 %halo.1.field_ref = f32[22,34,48]{2,1,0:T(8,128)} custom-call(f32[384,48]{1,0:T(8,128)} %reshape.95.own_ref), custom_call_target="tpu_custom_call" | custom-call | tf_op jit(solution)/shard_map/halo/pallas_call | solution.py:546
  16.5 1.7 %copy.18.k2_ref = bf16[864,32]{1,0:T(8,128)(2,1)} copy(bf16[864,32]{0,1:T(8,128)(2,1)} %param.12) | data formatting | bytes 110592 | tf_op args[5]
  18.1 21.3 %forward.1 = (f32[144,128]{1,0:T(8,128)}, f32[16,32,1536]{2,1,0:T(8,128)}, f32[18,32,1536]{2,1,0:T(8,128)}, bf16[16,32,1536]{2,1,0:T(8,128)(2,1)}, bf16[16,32,15...) custom-call(f32[22,34,48]{2,1,0:T(8,128)} %halo.1.field_ref, bf16[27,32]{1,0:T(8,128)(2,1)} %k1_ref.1, ...), custom_call_target="tpu_custom_call" | custom-call | tf_op jit(solution)/shard_map/forward/pallas_call | solution.py:561
  39.5 0.1 mul.36
  39.6 0.6 add.60.slot_ref
  40.1 1.5 %reshape.87.target_ref = s32[144,128]{1,0:T(8,128)} reshape(s32[16,1152]{1,0:T(8,128)} %param.9) | data formatting | bytes 147456 | tf_op jit(solution)/shard_map/reshape | solution.py:613
  41.6 1.5 %reshape.88.count_ref = s32[144,128]{1,0:T(8,128)} reshape(s32[16,1152]{1,0:T(8,128)} %param.8) | data formatting | bytes 147456 | tf_op jit(solution)/shard_map/reshape | solution.py:614
  43.2 27.6 %tiles.1 = (f32[144,128]{1,0:T(8,128)}, f32[1,128]{1,0:T(1,128)}, f32[192,128]{1,0:T(8,128)}, f32[192,128]{1,0:T(8,128)}) custom-call(f32[144,128]{1,0:T(8,128)} %get-tuple-element.19.rate_ref, s32[144,128]{1,0:T(8,128)} %reshape.87.target_ref, s32[144,128]{1,0:T(8,128)} %reshape.88.count_ref, s32[1,144]{1,0:T(1,128)} %add.60.slot_ref, f32[13,128]{1,0:T(8,128)} %pad.4.land_ref), custom_call_target="tpu_custom_call" | custom-call | tf_op jit(solution)/shard_map/tiles/pallas_call | solution.py:589
  70.8 1.0 reshape.90
  71.8 0.2 rev.3
  72.0 0.8 copy.19
  72.8 0.0 copy-start
  72.8 30.9 %backward.1.in_ref = f32[928,32]{1,0:T(8,128)} custom-call(f32[192,128]{1,0:T(8,128)} %get-tuple-element.21.main_ref, f32[192,128]{1,0:T(8,128)} %get-tuple-element.22.side_ref, f32[16,32,1536]{2,1,0:T(8,128)} %get-tuple-element.23.pre1_ref, f32[18,32,1536]{2,1,0:T(8,128)} %get-tuple-element.24.pre2_ref, bf16[16,32,1536]{2,1,0:T(8,128)(2,1)} %get-tuple-element.25.h1_ref, ...), custom_call_target="tpu_custom_call" | custom-call | tf_op jit(solution)/shard_map/backward/pallas_call | solution.py:619
  103.7 16.6 %sum.1 = (f32[27,32]{1,0:T(8,128)}, f32[864,32]{1,0:T(8,128)}, f32[27,32]{1,0:T(8,128)}, f32[1,1]{1,0:T(1,128)}) custom-call(f32[928,32]{1,0:T(8,128)} %backward.1.in_ref, f32[1,128]{1,0:T(1,128)} %get-tuple-element.28.loss_ref), custom_call_target="tpu_custom_call" | custom-call | tf_op jit(solution)/shard_map/sum/pallas_call | solution.py:642
  120.3 1.8 %copy.20 = f32[864,32]{0,1:T(8,128)} copy(f32[864,32]{1,0:T(8,128)} %get-tuple-element.46) | data formatting | bytes 221184
  122.2 1.4 %reshape.93 = f32[864,1]{0,1:T(1,128)} reshape(f32[27,32]{1,0:T(8,128)} %get-tuple-element.32) | data formatting | bytes 6912 | tf_op jit(solution)/shard_map/reshape | solution.py:668
  123.5 0.0 copy-done
  123.5 0.6 reshape.89
  124.8 1.3 %copy.24 = f32[27,32]{1,0:T(8,128)} copy(f32[27,32]{1,0:T(8,128)} %get-tuple-element.58) | data formatting | bytes 6912
  (2 shorter events, 0.0 us)
Async XLA Ops:
  72.8 50.7 %copy-start = (f32[144,128]{1,0:T(8,128)S(1)}, f32[144,128]{1,0:T(8,128)}, u32[]{:S(2)}) copy-start(f32[144,128]{1,0:T(8,128)} %get-tuple-element.20) | copy-start | bytes 221188
